TPU v7x, 128 devices: a whole 4x4x4 slice. The times are simulated.
128 devices in a mesh: blk: 16 (over y_hi, x, core), narrow: 8 (over z, y_lo).
Axes of the slice: x: 4, y: 4 (y_hi: 2, y_lo: 2; y = y_hi * 2 + y_lo), z: 4, core: 2. Of those that a mesh axis runs over, the one named last changes fastest.
Arguments:
- features: float32 [256, 131072], P('narrow', 'blk'), may hold values from -6 to 6
- degrees: int32 [131072], P('blk'), may hold values from 1 to 400
- tile_values: float32 [4096, 128, 128], P('blk'), may hold values from -24 to 24
- tile_list: int32 [16, 16, 3, 16], P('blk'), may hold values from 0 to 255, as said below
- tile_count: int32 [16, 16], P('blk'), may hold values from 0 to 16, as said below
- hub_local: int32 [16, 8], P('blk'), may hold values from 0 to 8191
- hub_weights: float32 [128, 131072], P(None, 'blk'), may hold values from -12 to 12
- weight: float32 [256, 256], replicated, may hold values from -0.375 to 0.375
- out_bias: float32 [256], replicated, may hold values from -3 to 3
Outputs:
- layer_out: float32 [256, 131072], P('narrow', 'blk')
Inputs may be any that keep to these rules, and one draw needn't show every extreme that they name: `tile_list`: entries [:, :, 0, :] and [:, :, 1, :] lie below 64; for each target device the entries [d, :, 2, :] are the numbers 0 to 255, each once. `tile_count`: every target device has at least one source device with exactly 16 live slots.
All inputs are finite; a program needn't handle non-finite values.
Results may differ from a plain program's by a relative error of at most 0.0003.
Values sent between devices are 32-bit elements; how exact they have to be, the bound alone decides.
A program may use at most 128 MiB of HBM per device.

v0:
```python
import jax
import jax.numpy as jnp
from jax import lax
from jax.sharding import PartitionSpec as P

TILE = 128
SLOTS = 16


def tile_products(src_blocks, row_ids, tile_ids, is_live, tile_values, blocks):
    tile_total = tile_values.shape[0]
    placing = jnp.arange(tile_total, dtype=jnp.int32)[:, None] == tile_ids[None, :]
    src_by_tile = jnp.einsum(
        "csj,ts->ctj", src_blocks, placing.astype(jnp.float32), precision=lax.Precision.HIGHEST
    )
    row_by_tile = jnp.sum(jnp.where(placing, row_ids[None, :], 0), axis=1)
    live_by_tile = jnp.any(placing & is_live[None, :], axis=1)
    products = jnp.einsum("ctj,tij->cti", src_by_tile, tile_values, precision=lax.Precision.HIGHEST)
    block_ids = jnp.arange(blocks, dtype=jnp.int32)
    chooser = ((row_by_tile[:, None] == block_ids[None, :]) & live_by_tile[:, None]).astype(
        jnp.float32
    )
    return jnp.einsum("cti,tr->cri", products, chooser, precision=lax.Precision.HIGHEST)


def body(
    features, degrees, tile_values, tile_list, tile_count, hub_local, hub_weights, weight, out_bias
):
    cols_dev = features.shape[0]
    node_dev = features.shape[1]
    blocks = node_dev // TILE
    inv_root = lax.rsqrt(degrees.astype(jnp.float32))
    scaled = features * inv_root[None, :]
    tile_lists = tile_list[0]
    slot_counts = tile_count[0]
    owner_count = tile_lists.shape[0]
    slot_pos = jnp.arange(SLOTS, dtype=jnp.int32)
    is_live = (slot_pos[None, :] < slot_counts[:, None]).reshape(-1)
    row_ids = tile_lists[:, 0, :].reshape(-1)
    tile_ids = tile_lists[:, 2, :].reshape(-1)
    shard_piece = lax.all_gather(scaled, "blk", axis=1, tiled=True)
    first_row = jnp.int32(0)
    piece_len = shard_piece.shape[1]
    owner_span = piece_len // node_dev
    first_owner = jnp.clip(first_row // node_dev, 0, owner_count - owner_span)
    owner_ids = first_owner + jnp.arange(owner_span, dtype=jnp.int32)
    col_ids = (owner_ids[:, None] * blocks + tile_lists[:, 1, :]).reshape(-1)
    padded_blocks = piece_len // TILE + 2
    offset = first_row % TILE
    buffer = jnp.zeros((cols_dev, padded_blocks * TILE), jnp.float32)
    buffer = lax.dynamic_update_slice_in_dim(buffer, shard_piece, offset, 1)
    block_pos = jnp.arange(padded_blocks, dtype=jnp.int32)
    selector = (col_ids[:, None] == block_pos[None, :]).astype(jnp.float32)
    picked = jnp.einsum(
        "cbj,sb->csj",
        buffer.reshape(cols_dev, padded_blocks, TILE),
        selector,
        precision=lax.Precision.HIGHEST,
    )
    tile_sum = tile_products(picked, row_ids, tile_ids, is_live, tile_values, blocks)
    hub_pick = (hub_local[0][:, None] == jnp.arange(node_dev, dtype=jnp.int32)[None, :]).astype(
        jnp.float32
    )
    hub_cols = jnp.einsum("cn,hn->ch", scaled, hub_pick, precision=lax.Precision.HIGHEST)
    hub_all = lax.all_gather(hub_cols, "blk", axis=1, tiled=True)
    hub_sum = jnp.dot(hub_all, hub_weights, precision=lax.Precision.HIGHEST)
    aggregated = inv_root[None, :] * (tile_sum.reshape(cols_dev, node_dev) + hub_sum + scaled)
    regrouped = lax.all_to_all(aggregated, "narrow", split_axis=1, concat_axis=0, tiled=True)
    mixed_out = jax.nn.relu(
        jnp.dot(weight.T, regrouped, precision=lax.Precision.HIGHEST) + out_bias[:, None]
    )
    return lax.all_to_all(mixed_out, "narrow", split_axis=0, concat_axis=1, tiled=True)


def solution(mesh):
    return jax.shard_map(
        body,
        mesh=mesh,
        in_specs=(
            P("narrow", "blk"),
            P("blk"),
            P("blk", None, None),
            P("blk", None, None, None),
            P("blk", None),
            P("blk", None),
            P(None, "blk"),
            P(),
            P(),
        ),
        out_specs=P("narrow", "blk"),
        check_vma=False,
    )
```

profile of v0, /device:TPU:1, one launch (start us, length us, event | category | flops | bytes accessed | tf_op | source)
XLA Modules:
  0.0 253.3 jit_solution(1221354240615733297)
XLA Ops:
  6.5 0.0 copy-start
  6.5 0.0 all-gather.2.cloned.1.call-start
  6.5 0.8 convert_rsqrt_fusion
  7.4 2.3 broadcast_multiply_fusion
  9.6 0.0 all-gather.2.cloned.1.call-update
  9.7 0.7 fusion.31
  10.4 0.1 squeeze.7
  10.5 0.1 add.38
  10.5 0.1 add.39
  10.6 0.1 eq.59
  10.7 0.1 broadcast_in_dim.14
  10.8 0.7 iota_compare_fusion.5
  11.5 0.1 lt.31
  11.6 1.8 fusion.23
  13.5 26.1 %all_gather.7 = f32[32,128]{0,1:T(8,128)S(1)} all-gather(f32[32,8]{0,1:T(8,128)S(1)} %fusion.23), channel_id=1, replica_groups=mesh['blk'=16,'narrow'=8] {'blk'}, dimensions={1}, use_global_device_ids=true | all-gather | bytes 17408 | tf_op jit(solution)/shard_map/all_gather | solution.py:65
  39.6 0.1 fusion.21
  39.7 0.1 select_reduce_fusion
  39.8 84.0 %all-gather.2.cloned.1.call-done = f32[32,131072]{1,0:T(8,128)} async-done(((f32[32,8192]{1,0:T(8,128)}), f32[32,131072]{1,0:T(8,128)}) %all-gather.2.cloned.1.call-update) | async-done | bytes 16777232 | tf_op jit(solution)/shard_map/all_gather | solution.py:41
  123.8 11.3 %dynamic_update_slice.3 = f32[32,131328]{1,0:T(8,128)} pad(f32[32,131072]{1,0:T(8,128)} %all-gather.2.cloned.1.call-done, f32[]{:T(128)} %constant.42.clone.1), padding=0_0x0_256 | pad | bytes 33587204 | tf_op jit(solution)/shard_map/dynamic_update_slice | solution.py:51
  135.1 19.0 %reshape.50 = f32[32,1026,128]{2,1,0:T(8,128)} reshape(f32[32,131328]{1,0:T(8,128)} %dynamic_update_slice.3) | data formatting | bytes 33619968 | tf_op jit(solution)/shard_map/reshape | solution.py:56
  154.1 13.2 %fusion.16 = f32[256,32,128]{2,0,1:T(8,128)S(1)} fusion(f32[32,1026,128]{2,1,0:T(8,128)} %reshape.50, s32[256]{0:T(256)S(1)} %add.40), kind=kOutput, calls=%fused_computation.15 | convolution fusion | flops 12910329856 | bytes 21005312 | tf_op jit(solution)/shard_map/cbj,sb->csj/dot_general | solution.py:54
  167.3 2.6 %fusion.11 = f32[32,256,128]{2,1,0:T(8,128)S(1)} fusion(f32[256,32,128]{2,0,1:T(8,128)S(1)} %fusion.16, s32[256]{0:T(256)S(1)} %eq.59), kind=kOutput, calls=%fused_computation.10 | convolution fusion | flops 3221291008 | bytes 8389632 | tf_op jit(solution)/shard_map/csj,ts->ctj/dot_general | solution.py:13
  170.0 30.2 %fusion.8 = f32[32,256,128]{2,0,1:T(8,128)S(1)} fusion(f32[256,128,128]{2,1,0:T(8,128)} %param.11, f32[32,256,128]{2,1,0:T(8,128)S(1)} %fusion.11), kind=kOutput, calls=%fused_computation.9 | convolution fusion | flops 1610612736 | bytes 25165824 | tf_op jit(solution)/shard_map/ctj,tij->cti/dot_general | solution.py:18
  200.2 0.0 copy-start.1
  200.2 0.0 copy-start.2
  200.2 4.1 %fusion.4 = f32[64,32,128]{2,0,1:T(8,128)S(1)} fusion(f32[32,256,128]{2,0,1:T(8,128)S(1)} %fusion.8, s32[256]{0:T(256)S(1)} %select_reduce_fusion, pred[256]{0:T(512)(128)(4,1)S(1)} %fusion.21), kind=kOutput, calls=%fused_computation.5 | convolution fusion | flops 805339136 | bytes 5244160 | tf_op jit(solution)/shard_map/cti,tr->cri/dot_general | solution.py:23
  204.3 0.0 copy-done.1
  204.3 0.0 copy-done.2
  204.3 0.0 copy-start.3
  204.3 2.8 %fusion.1 = f32[32,8192]{1,0:T(8,128)S(1)} fusion(f32[32,8192]{1,0:T(8,128)S(1)} %copy-done.1, f32[32,128]{0,1:T(8,128)S(1)} %all_gather.7, f32[128,8192]{1,0:T(8,128)S(1)} %copy-done.2, f32[4,8,64,128]{3,2,1,0:T(8,128)S(1)} %bitcast.52, f32[8192]{0:T(1024)S(1)} %convert_rsqrt_fusion), kind=kOutput, calls=%fused_computation.2 | convolution fusion | flops 403439616 | bytes 7389184 | tf_op jit(solution)/shard_map/dot_general | solution.py:66
  207.2 0.1 copy.28
  207.2 19.0 %all_to_all.38 = f32[32,8,1024]{2,0,1:T(8,128)S(1)} all-to-all(f32[32,8,1024]{2,0,1:T(8,128)S(1)} %bitcast.53), channel_id=1, replica_groups=mesh['blk'=16,'narrow'=8] {'narrow'}, dimensions={1} | all-to-all | bytes 2097152 | tf_op jit(solution)/shard_map/all_to_all | solution.py:68
  226.2 0.0 copy-done
  226.2 0.0 copy-done.3
  226.2 1.1 fusion.14
  227.3 18.0 %all_to_all.39 = f32[8,32,1024]{2,1,0:T(8,128)S(1)} all-to-all(f32[8,32,1024]{2,1,0:T(8,128)S(1)} %bitcast.55), channel_id=1, replica_groups=mesh['blk'=16,'narrow'=8] {'narrow'}, dimensions={0} | all-to-all | bytes 2097152 | tf_op jit(solution)/shard_map/all_to_all | solution.py:72
  245.3 1.1 copy.18
  (2 shorter events, 0.0 us)
Async XLA Ops:
  6.5 219.7 %copy-start = (f32[256,256]{1,0:T(8,128)S(1)}, f32[256,256]{1,0:T(8,128)}, u32[]{:S(2)}) copy-start(f32[256,256]{1,0:T(8,128)} %param.16) | copy-start | bytes 786436
  6.5 117.3 %all-gather.2.cloned.1.call-start = ((), (), s32[]{:S(2)}) async-start(), calls=%async_computation.2 | async-start | bytes 17825792 | tf_op jit(solution)/shard_map/all_gather | solution.py:41
  200.2 4.1 %copy-start.1 = (f32[32,8192]{1,0:T(8,128)S(1)}, f32[32,8192]{1,0:T(8,128)}, u32[]{:S(2)}) copy-start(f32[32,8192]{1,0:T(8,128)} %broadcast_multiply_fusion) | copy-start | bytes 3145732
  200.2 4.1 %copy-start.2 = (f32[128,8192]{1,0:T(8,128)S(1)}, f32[128,8192]{1,0:T(8,128)}, u32[]{:S(2)}) copy-start(f32[128,8192]{1,0:T(8,128)} %param.15) | copy-start | bytes 12582916
  204.3 21.9 %copy-start.3 = (f32[256]{0:T(256)S(1)}, f32[256]{0:T(256)}, u32[]{:S(2)}) copy-start(f32[256]{0:T(256)} %param.17) | copy-start | bytes 3076
Sparse Core Ops, SparseCore 0:
  9.8 113.9 all-gather.1
where the time goes:
time: 254 us; the launch traced here: 253 us
  waiting for transfers between devices  84 us (33%)
  blocking collectives  63.1 us (25%)
  matrix products  55.9 us (22%)
  local copies, waits for them, and re-layouts  32.7 us (13%)
  between operations  13.5 us (5%)
  other arithmetic  4.07 us (2%)
    all_gather x1, waiting for transfers between devices, body(): shard_piece = lax.all_gather(scaled, 'blk', axis=1, tiled=True)  84 us
    dot_general x1, matrix products, tile_products(): jnp.einsum('ctj,tij->cti', src_by_tile, tile_values, precision=lax.Precis...  30.2 us
    all_gather x1, blocking collectives, body(): hub_all = lax.all_gather(hub_cols, 'blk', axis=1, tiled=True)  26.1 us
    reshape x1, local copies, waits for them, and re-layouts, body(): buffer.reshape(cols_dev, padded_blocks, TILE)  19 us
    all_to_all x1, blocking collectives, body(): lax.all_to_all(aggregated, 'narrow', split_axis=1, concat_axis=0, tiled=T...  19 us
    all_to_all x1, blocking collectives, body(): lax.all_to_all(mixed_out, 'narrow', split_axis=0, concat_axis=1, tiled=True)  18 us
    dot_general x1, matrix products, body(): jnp.einsum('cbj,sb->csj', buffer.reshape(cols_dev, padded_blocks, TILE),...  13.2 us
    dynamic_update_slice x1, local copies, waits for them, and re-layouts, body(): buffer = lax.dynamic_update_slice_in_dim(buffer, shard_piece, offset, 1)  11.3 us
  transfers between devices with their start and end apart: 1, of which 1 were waited for; matrix products, arithmetic and copies ran while one was open for 2% of the time, Pallas kernels for 0%

commit v1 on v0

v1 whole, which is shorter than its diff:
```python
import functools

import jax
import jax.numpy as jnp
from jax import lax
from jax.experimental import pallas as pl
from jax.experimental.pallas import tpu as pltpu
from jax.sharding import PartitionSpec as P

TILE = 128
SLOTS = 16
F = 4
BLOCKS = 64
TV = 256
GROUP = 8
MESH = pl.DeviceIdType.MESH
ROW = ((1, 0), (3, 0), (1, 1), (3, 1), (2, 0), (2, 1), (0, 1))
NARROW = ((1, 0), (3, 0), (0, 1), (2, 0), (1, 1), (3, 1), (2, 1))


def split(x):
    hi = x.astype(jnp.bfloat16)
    lo = (x - hi.astype(jnp.float32)).astype(jnp.bfloat16)
    return hi, lo


def nt_dot(a, b):
    return lax.dot_general(a, b, (((1,), (1,)), ((), ())), preferred_element_type=jnp.float32)


def nn_dot(a, b):
    return jnp.dot(a, b, preferred_element_type=jnp.float32)


def exchange_kernel(
    feat, deg, weight, cols, hubs,
    recv, y_out, hub_out,
    xt, ysend, ya, yb, yc, yd, pa, pb, pc, pd, own_b, par_b, lists_v, lists_s, hub_v,
    s1, r1, s2, r2, sy, ry, sl, rl, sh, rh, so, sp, rr, loc,
):
    y4, yp = (ya, yb, yc, yd), (pa, pb, pc, pd)
    blk = lax.axis_index("blk")
    nar = lax.axis_index("narrow")
    yh, x, core = blk // 8, (blk // 2) % 4, blk % 2
    z, yl = nar // 2, nar % 2
    partner = (1 - yh) * 8 + x * 2 + core

    def row_peer(step, other):
        return yh * 8 + lax.rem(x + step, 4) * 2 + lax.rem(core + other, 2)

    def narrow_peer(step, other):
        return lax.rem(z + step, 4) * 2 + lax.rem(yl + other, 2)

    bar = pltpu.get_barrier_semaphore()
    for j in range(1, 16):
        pl.semaphore_signal(bar, inc=1, device_id=(lax.rem(blk + j, 16), nar), device_id_type=MESH)
    for step, other in NARROW:
        pl.semaphore_signal(
            bar, inc=1, device_id=(blk, narrow_peer(step, other)), device_id_type=MESH
        )
    pl.semaphore_wait(bar, 22)

    def send1(n, to):
        return pltpu.make_async_remote_copy(
            src_ref=feat.at[:, pl.ds(pl.multiple_of(to * 1024, 1024), 1024)],
            dst_ref=xt.at[pl.ds(pl.multiple_of(n * 32, 32), 32), :],
            send_sem=s1.at[to], recv_sem=r1.at[n],
            device_id=(blk, to), device_id_type=MESH,
        )

    for step, other in NARROW:
        send1(nar, narrow_peer(step, other)).start()
    own1 = pltpu.make_async_copy(
        feat.at[:, pl.ds(pl.multiple_of(nar * 1024, 1024), 1024)],
        xt.at[pl.ds(pl.multiple_of(nar * 32, 32), 32), :], loc.at[0],
    )
    own1.start()

    def send_list(step, other):
        slot = step * 2 + other
        return pltpu.make_async_remote_copy(
            src_ref=cols, dst_ref=lists_v.at[slot], send_sem=sl.at[slot], recv_sem=rl.at[slot],
            device_id=(row_peer(4 - step, other), nar), device_id_type=MESH,
        )

    for step, other in ROW:
        send_list(step, other).start()
    lists_v[0] = cols[...]
    for step, other in ROW:
        send_list(step, other).wait()
    to_smem = pltpu.make_async_copy(lists_v, lists_s, loc.at[1])
    to_smem.start()

    wh, wl = split(weight[...].T)
    inv = lax.rsqrt(deg[pl.ds(pl.multiple_of(nar * 8, 8), 8), :].astype(jnp.float32))
    to_smem.wait()
    own1.wait()
    for step, other in NARROW:
        send1(narrow_peer(step, other), narrow_peer(step, other)).wait_recv()

    for b in range(8):
        xh, xl = split(xt[:, b * TILE : (b + 1) * TILE])
        y = nn_dot(wh, xh) + nn_dot(wl, xh) + nn_dot(wh, xl)
        y = y * inv[b : b + 1, :]
        for n in range(8):
            for f in range(F):
                row = n * 32 + f * 8
                ysend[f, n, b] = y[row : row + 8, :]

    def send2(f, n, to):
        return pltpu.make_async_remote_copy(
            src_ref=ysend.at[f, to],
            dst_ref=y4[f].at[pl.ds(pl.multiple_of(n * 8, 8), 8)],
            send_sem=s2.at[f, to], recv_sem=r2.at[f, n],
            device_id=(blk, to), device_id_type=MESH,
        )

    def own2(f):
        return pltpu.make_async_copy(
            ysend.at[f, nar], y4[f].at[pl.ds(pl.multiple_of(nar * 8, 8), 8)], loc.at[2 + f]
        )

    for f in range(F):
        for step, other in NARROW:
            send2(f, nar, narrow_peer(step, other)).start()
        own2(f).start()

    def send_y(f):
        return pltpu.make_async_remote_copy(
            src_ref=y4[f], dst_ref=yp[f], send_sem=sy.at[f], recv_sem=ry.at[f],
            device_id=(partner, nar), device_id_type=MESH,
        )

    def send_blocks(buf, sem, f, source, step, other):
        slot = step * 2 + other
        return pltpu.make_async_remote_copy(
            src_ref=buf.at[f, slot], dst_ref=recv.at[f, source],
            send_sem=sem.at[f, slot], recv_sem=rr.at[f, source],
            device_id=(row_peer(step, other), nar), device_id_type=MESH,
        )

    def keep_blocks(buf, f, source, sem):
        return pltpu.make_async_copy(buf.at[f, 0], recv.at[f, source], sem)

    def pack(src, buf, f, source, slot):
        for k in range(SLOTS):
            c = lists_s[slot, source // 8, lax.rem(source, 8) * SLOTS + k]
            buf[f, slot, k] = src[f][c]

    for f in range(F):
        own2(f).wait()
        for step, other in NARROW:
            n = narrow_peer(step, other)
            send2(f, n, n).wait_recv()
        send_y(f).start()
        for step, other in ROW:
            pack(y4, own_b, f, blk, step * 2 + other)
            send_blocks(own_b, so, f, blk, step, other).start()
        pack(y4, own_b, f, blk, 0)
        keep_blocks(own_b, f, blk, loc.at[6 + f]).start()

    lane = lax.broadcasted_iota(jnp.int32, (8, TILE), 1)
    hub = jnp.zeros((8, TILE), jnp.float32)
    for h in range(8):
        node = hubs[h]
        here = lane == lax.rem(node, TILE)
        for f in range(F):
            column = jnp.sum(jnp.where(here, y4[f][node // TILE], 0.0), axis=1, keepdims=True)
            hub = jnp.where(lane == f * 8 + h, column, hub)
    hub_v[...] = hub

    def send_hub(source, to):
        return pltpu.make_async_remote_copy(
            src_ref=hub_v, dst_ref=hub_out.at[source], send_sem=sh.at[to], recv_sem=rh.at[source],
            device_id=(to, nar), device_id_type=MESH,
        )

    for j in range(1, 16):
        send_hub(blk, lax.rem(blk + j, 16)).start()
    keep_hub = pltpu.make_async_copy(hub_v, hub_out.at[blk], loc.at[14])
    keep_hub.start()
    keep_y = [pltpu.make_async_copy(y4[f], y_out.at[f], loc.at[15 + f]) for f in range(F)]
    for f in range(F):
        keep_y[f].start()

    for f in range(F):
        send_y(f).wait_recv()
        for step, other in ROW:
            pack(yp, par_b, f, partner, step * 2 + other)
            send_blocks(par_b, sp, f, partner, step, other).start()
        pack(yp, par_b, f, partner, 0)
        keep_blocks(par_b, f, partner, loc.at[10 + f]).start()

    for f in range(F):
        for step, other in ROW:
            peer = row_peer(step, other)
            send_blocks(own_b, so, f, peer, step, other).wait()
            other_row = lax.rem(peer + 8, 16)
            send_blocks(par_b, sp, f, other_row, step, other).wait()
        keep_blocks(own_b, f, blk, loc.at[6 + f]).wait()
        keep_blocks(par_b, f, partner, loc.at[10 + f]).wait()
        send_y(f).wait_send()
        for step, other in NARROW:
            n = narrow_peer(step, other)
            send2(f, n, n).wait_send()
    for step, other in NARROW:
        n = narrow_peer(step, other)
        send1(n, n).wait_send()
    for j in range(1, 16):
        peer = lax.rem(blk + j, 16)
        send_hub(peer, peer).wait()
    keep_hub.wait()
    for f in range(F):
        keep_y[f].wait()


def exchange(feat, deg, weight, cols, hubs):
    f32 = jnp.float32
    dma = pltpu.SemaphoreType.DMA
    vmem = pl.BlockSpec(memory_space=pltpu.VMEM)
    smem = pl.BlockSpec(memory_space=pltpu.SMEM)
    hbm = pl.BlockSpec(memory_space=pl.ANY)
    return pl.pallas_call(
        exchange_kernel,
        out_shape=(
            jax.ShapeDtypeStruct((F, 16, SLOTS, 8, TILE), f32),
            jax.ShapeDtypeStruct((F, BLOCKS, 8, TILE), f32),
            jax.ShapeDtypeStruct((16, 8, TILE), f32),
        ),
        in_specs=[hbm, vmem, vmem, vmem, smem],
        out_specs=(hbm, hbm, hbm),
        scratch_shapes=[
            pltpu.VMEM((256, 1024), f32),
            pltpu.VMEM((F, 8, 8, 8, TILE), f32),
            *[pltpu.VMEM((BLOCKS, 8, TILE), f32)] * 8,
            pltpu.VMEM((F, 8, SLOTS, 8, TILE), f32),
            pltpu.VMEM((F, 8, SLOTS, 8, TILE), f32),
            pltpu.VMEM((8, 8, TILE), jnp.int32),
            pltpu.SMEM((8, 8, TILE), jnp.int32),
            pltpu.VMEM((8, TILE), f32),
            dma((8,)), dma((8,)),
            dma((F, 8)), dma((F, 8)),
            dma((F,)), dma((F,)),
            dma((8,)), dma((8,)),
            dma((16,)), dma((16,)),
            dma((F, 8)), dma((F, 8)), dma((F, 16)),
            dma((20,)),
        ],
        compiler_params=pltpu.CompilerParams(
            collective_id=0, has_side_effects=True, vmem_limit_bytes=32 * 2**20
        ),
    )(feat, deg, weight, cols, hubs)


def tile_kernel(
    recv, y4, hub_in, deg, bias, hub_w, lists, counts, tiles,
    out,
    acc, tbuf, hw_buf, src_s, row_s, buf_s, sem, hw_sem,
):
    fetch_hw = pltpu.make_async_copy(hub_w, hw_buf, hw_sem)
    fetch_hw.start()

    def fetch(t, pos):
        return pltpu.make_async_copy(tiles.at[t], tbuf.at[pos], sem.at[pos])

    def source(o, pos):
        def slot(k, pos):
            src_s[pos] = o * SLOTS + k
            row_s[pos] = lists[o * 3, k]
            buf_s[pos] = pos
            fetch(lists[o * 3 + 2, k], pos).start()
            return pos + 1

        return lax.fori_loop(0, counts[0, o], slot, pos)

    live = lax.fori_loop(0, 16, source, jnp.int32(0))
    for j in range(GROUP):
        src_s[live + j] = 0
        row_s[live + j] = BLOCKS
        buf_s[live + j] = 0

    lane = lax.broadcasted_iota(jnp.int32, (8, TILE), 1)
    hub = []
    for f in range(F):
        total = jnp.zeros((8, TILE), jnp.float32)
        for o in range(16):
            moved = pltpu.roll(hub_in[o], (o * 8 - f * 8) % TILE, 1)
            total = jnp.where(lane // 8 == o, moved, total)
        hub.append(total)
    gh, gl = split(jnp.concatenate(hub, axis=0))
    g2 = jnp.concatenate([gh, gl], axis=0)
    fetch_hw.wait()

    def base(i, carry):
        hh, hl = split(hw_buf[:, pl.ds(pl.multiple_of(i * 512, 512), 512)])
        p = nn_dot(g2, hh)
        p = p[:32] + p[32:] + nn_dot(gh, hl)
        for b in range(4):
            for f in range(F):
                acc[i * 4 + b, f] = (
                    p[f * 8 : f * 8 + 8, b * TILE : (b + 1) * TILE] + y4[f, i * 4 + b]
                )
        return carry

    lax.fori_loop(0, 16, base, 0)

    def group(g, carry):
        first = g * GROUP
        for j in range(GROUP):
            @pl.when(first + j < live)
            def _():
                fetch(0, first + j).wait()

        products = []
        for j in range(GROUP):
            s = src_s[first + j]
            xs = jnp.concatenate([recv[f, s] for f in range(F)], axis=0)
            xh, xl = split(xs)
            th, tl = split(tbuf[buf_s[first + j]])
            p = nt_dot(jnp.concatenate([xh, xl], axis=0), th)
            products.append(p[:32] + p[32:] + nt_dot(xh, tl))
        for j in range(GROUP):
            r = row_s[first + j]
            for f in range(F):
                acc[r, f] += products[j][f * 8 : f * 8 + 8, :]
        return carry

    lax.fori_loop(0, (live + GROUP - 1) // GROUP, group, 0)

    def finish(i, carry):
        inv = lax.rsqrt(deg[pl.ds(pl.multiple_of(i * 8, 8), 8), :].astype(jnp.float32))
        for b in range(8):
            for f in range(F):
                value = acc[i * 8 + b, f] * inv[b : b + 1, :] + bias[f * 8 : f * 8 + 8, :]
                out[f * 8 : f * 8 + 8, pl.ds(pl.multiple_of((i * 8 + b) * TILE, TILE), TILE)] = (
                    jnp.maximum(value, 0.0)
                )
        return carry

    lax.fori_loop(0, 8, finish, 0)


def tile_sums(recv, y4, hub_in, deg, bias, hub_w, lists, counts, tiles):
    f32 = jnp.float32
    vmem = pl.BlockSpec(memory_space=pltpu.VMEM)
    smem = pl.BlockSpec(memory_space=pltpu.SMEM)
    hbm = pl.BlockSpec(memory_space=pl.ANY)
    return pl.pallas_call(
        tile_kernel,
        out_shape=jax.ShapeDtypeStruct((32, BLOCKS * TILE), f32),
        in_specs=[vmem, vmem, vmem, vmem, vmem, hbm, smem, smem, hbm],
        out_specs=vmem,
        scratch_shapes=[
            pltpu.VMEM((BLOCKS + 1, F, 8, TILE), f32),
            pltpu.VMEM((TV, TILE, TILE), f32),
            pltpu.VMEM((128, BLOCKS * TILE), f32),
            pltpu.SMEM((TV + GROUP,), jnp.int32),
            pltpu.SMEM((TV + GROUP,), jnp.int32),
            pltpu.SMEM((TV + GROUP,), jnp.int32),
            pltpu.SemaphoreType.DMA((TV,)),
            pltpu.SemaphoreType.DMA,
        ],
        compiler_params=pltpu.CompilerParams(vmem_limit_bytes=48 * 2**20),
    )(recv, y4, hub_in, deg, bias, hub_w, lists, counts, tiles)


def body(
    features, degrees, tile_values, tile_list, tile_count, hub_local, hub_weights, weight, out_bias
):
    deg = degrees.reshape(BLOCKS, TILE)
    cols = jnp.pad(tile_list[0, :, 1, :].reshape(2, TILE), ((0, 6), (0, 0)))
    recv, y4, hub = exchange(features, deg, weight, cols, hub_local.reshape(8))
    mine = lax.dynamic_slice_in_dim(out_bias, lax.axis_index("narrow") * 32, 32)
    bias = jnp.broadcast_to(mine[:, None], (32, TILE))
    return tile_sums(
        recv.reshape(F, 16 * SLOTS, 8, TILE), y4, hub, deg, bias, hub_weights,
        tile_list.reshape(48, SLOTS), tile_count, tile_values,
    )


def solution(mesh):
    return jax.shard_map(
        body,
        mesh=mesh,
        in_specs=(
            P("narrow", "blk"),
            P("blk"),
            P("blk", None, None),
            P("blk", None, None, None),
            P("blk", None),
            P("blk", None),
            P(None, "blk"),
            P(),
            P(),
        ),
        out_specs=P("narrow", "blk"),
        check_vma=False,
    )
```

time: 254 us -> 103 us (0.41)
  Pallas kernels: 0 us -> 95 us
  waiting for transfers between devices: 84 us -> 0 us
  blocking collectives: 63.1 us -> 0 us
  matrix products: 55.9 us -> 0 us
  local copies, waits for them, and re-layouts: 32.7 us -> 7.37 us
  between operations: 13.5 us -> 0.04 us
  other arithmetic: 4.07 us -> 0 us
    pallas_call x0 -> x2, Pallas kernels: none -> 95 us  [the longest x1 78.5 us: exchange(): pl.pallas_call(exchange_kernel, out_shape=(jax.ShapeDtypeStruct((F, 16, S...]
    all_gather x1 -> x0, waiting for transfers between devices: 84 us -> none  [body(): shard_piece = lax.all_gather(scaled, 'blk', axis=1, tiled=True)]
    dot_general x7 -> x0, matrix products: 55.9 us -> none  [the longest x1 30.2 us: tile_products(): jnp.einsum('ctj,tij->cti', src_by_tile, tile_values, precision=lax.Precis...]
    all_to_all x2 -> x0, blocking collectives: 37 us -> none  [the longest x1 19 us: body(): lax.all_to_all(aggregated, 'narrow', split_axis=1, concat_axis=0, tiled=T...]
    all_gather x1 -> x0, blocking collectives: 26.1 us -> none  [body(): hub_all = lax.all_gather(hub_cols, 'blk', axis=1, tiled=True)]
    reshape x1, local copies, waits for them, and re-layouts: 19 us -> 0.02 us  [body(): tile_list.reshape(48, SLOTS)]
    dynamic_update_slice x1 -> x0, local copies, waits for them, and re-layouts: 11.3 us -> none  [body(): buffer = lax.dynamic_update_slice_in_dim(buffer, shard_piece, offset, 1)]
    unnamed x8 -> x13, local copies, waits for them, and re-layouts: 0.02 us -> 5.74 us
  transfers between devices with their start and end apart: 1 -> 0, of which waited for: 1 -> 0; matrix products, arithmetic and copies ran while one was open for 2% -> 0% of each run, Pallas kernels for 0% -> 0%
where the time goes in v1:
time: 103 us; the launch traced here: 102 us
  Pallas kernels  95 us (92%)
  local copies, waits for them, and re-layouts  7.37 us (7%)
    pallas_call x1, Pallas kernels, exchange(): pl.pallas_call(exchange_kernel, out_shape=(jax.ShapeDtypeStruct((F, 16, S...  78.5 us
    pallas_call x1, Pallas kernels, tile_sums(): pl.pallas_call(tile_kernel, out_shape=jax.ShapeDtypeStruct((32, BLOCKS *...  16.5 us
    unnamed x13, local copies, waits for them, and re-layouts  5.74 us

profile of v1, /device:TPU:1, one launch (start us, length us, event | category | flops | bytes accessed | tf_op | source)
XLA Modules:
  0.0 102.4 jit_solution(4163928985010372422)
XLA Ops:
  0.0 0.8 dynamic_slice.3
  0.8 0.7 slice.3
  1.4 0.1 reshape_squeeze.3
  1.5 0.1 broadcast_in_dim.2.bias
  1.6 0.8 copy.11
  2.4 0.0 copy-start
  2.4 1.2 %copy-done = f32[32,8192]{1,0:T(8,128)S(1)} copy-done((f32[32,8192]{1,0:T(8,128)S(1)}, f32[32,8192]{1,0:T(8,128)}, u32[]{:S(2)}) %copy-start) | copy-done | bytes 1048600
  3.6 0.0 copy-start.1
  3.6 0.9 copy-done.1
  4.6 0.0 copy-start.2
  4.6 0.8 copy-done.2
  5.3 0.0 copy-start.4
  5.3 0.7 copy-done.4
  6.0 78.5 %shard_map.91 = (f32[4,16,16,8,128]{4,3,2,1,0:T(8,128)S(1)}, f32[4,64,8,128]{3,2,1,0:T(8,128)S(1)}, f32[16,8,128]{2,1,0:T(8,128)S(1)}) custom-call(f32[32,8192]{1,0:T(8,128)S(1)} %copy-done, s32[64,128]{1,0:T(8,128)S(1)} %bitcast.8, f32[256,256]{1,0:T(8,128)S(1)} %copy-done.1, s32[8,128]{1,0:T(8,128)S(1)} %pad.4.cols, s32[8]{0:T(128)S(1)} %bitcast.10), custom_call_target="tpu_custom_call" | custom-call | tf_op jit(solution)/shard_map/pallas_call | solution.py:223
  84.5 0.0 copy-start.3
  84.5 0.7 copy-done.3
  85.2 0.0 copy-start.5
  85.2 0.7 copy-done.5
  85.9 16.5 %shard_map.92 = f32[32,8192]{1,0:T(8,128)} custom-call(f32[4,256,8,128]{3,2,1,0:T(8,128)S(1)} %bitcast.7, f32[4,64,8,128]{3,2,1,0:T(8,128)S(1)} %get-tuple-element.9.y4, f32[16,8,128]{2,1,0:T(8,128)S(1)} %get-tuple-element.10.hub_in, s32[64,128]{1,0:T(8,128)S(1)} %bitcast.9, f32[32,128]{1,0:T(8,128)S(1)} %broadcast_in_dim.2.bias, f32[128,8192]{1,0:T(8,128)} %hub_w.1, ...), custom_call_target="tpu_custom_call" | custom-call | tf_op jit(solution)/shard_map/pallas_call | solution.py:348
  (2 shorter events, 0.0 us)
Async XLA Ops:
  2.4 1.2 %copy-start = (f32[32,8192]{1,0:T(8,128)S(1)}, f32[32,8192]{1,0:T(8,128)}, u32[]{:S(2)}) copy-start(f32[32,8192]{1,0:T(8,128)} %feat.1) | copy-start | bytes 3145732
  3.6 0.9 copy-start.1
  4.6 0.8 copy-start.2
  5.3 0.7 copy-start.4
  84.5 0.8 copy-start.3
  85.2 0.7 copy-start.5

commit v2 on v1

v2 whole, which is shorter than its diff:
```python
import functools

import jax
import jax.numpy as jnp
from jax import lax
from jax.experimental import pallas as pl
from jax.experimental.pallas import tpu as pltpu
from jax.sharding import PartitionSpec as P

TILE = 128
SLOTS = 16
F = 4
BLOCKS = 64
TV = 256
MESH = pl.DeviceIdType.MESH
ROW = ((1, 0), (3, 0), (1, 1), (3, 1), (2, 0), (2, 1), (0, 1))
NARROW = ((1, 0), (3, 0), (0, 1), (2, 0), (1, 1), (3, 1), (2, 1))


def split(x):
    hi = x.astype(jnp.bfloat16)
    lo = (x - hi.astype(jnp.float32)).astype(jnp.bfloat16)
    return hi, lo


def nt_dot(a, b):
    return lax.dot_general(a, b, (((1,), (1,)), ((), ())), preferred_element_type=jnp.float32)


def nn_dot(a, b):
    return jnp.dot(a, b, preferred_element_type=jnp.float32)


def exchange_kernel(
    feat, deg, weight, lists, my_list, hubs, tiles, hub_w,
    prod_own, prod_par, base_out,
    xt, ysend, ya, yb, yc, yd, pa, pb, pc, pd, own_b, early_b, late_b,
    got_own, got_early, got_late, lists_v, lists_s, hub_v, hub_in, deg_v, w_v, t_v, hw_v,
    p_own, p_par, base,
    s1, r1, s2, r2, sy, ry, sl, rl, sh, rh, so, ro, se, re, sq, rq, loc,
):
    y4, yp = (ya, yb, yc, yd), (pa, pb, pc, pd)
    blk = lax.axis_index("blk")
    nar = lax.axis_index("narrow")
    yh, x, core = blk // 8, (blk // 2) % 4, blk % 2
    z, yl = nar // 2, nar % 2
    me = x * 2 + core
    partner = (1 - yh) * 8 + me

    def row_peer(step, other):
        return lax.rem(x + step, 4) * 2 + lax.rem(core + other, 2)

    def narrow_peer(step, other):
        return lax.rem(z + step, 4) * 2 + lax.rem(yl + other, 2)

    bar = pltpu.get_barrier_semaphore()
    for step, other in NARROW:
        pl.semaphore_signal(
            bar, inc=1, device_id=(blk, narrow_peer(step, other)), device_id_type=MESH
        )
    for step, other in ROW:
        pl.semaphore_signal(
            bar, inc=1, device_id=(yh * 8 + row_peer(step, other), nar), device_id_type=MESH
        )
    pl.semaphore_signal(bar, inc=1, device_id=(partner, nar), device_id_type=MESH)

    get_deg = pltpu.make_async_copy(deg, deg_v, loc.at[0])
    get_w = pltpu.make_async_copy(weight, w_v, loc.at[1])
    get_own = pltpu.make_async_copy(
        feat.at[:, pl.ds(pl.multiple_of(nar * 1024, 1024), 1024)],
        xt.at[pl.ds(pl.multiple_of(nar * 32, 32), 32), :], loc.at[2],
    )
    get_list = pltpu.make_async_copy(lists.at[0], lists_v.at[0], loc.at[3])
    get_t = pltpu.make_async_copy(tiles, t_v, loc.at[4])
    get_hw = pltpu.make_async_copy(hub_w, hw_v, loc.at[5])
    for copy in (get_w, get_deg, get_own, get_list):
        copy.start()
    pl.semaphore_wait(bar, 15)

    def send1(n, to):
        return pltpu.make_async_remote_copy(
            src_ref=feat.at[:, pl.ds(pl.multiple_of(to * 1024, 1024), 1024)],
            dst_ref=xt.at[pl.ds(pl.multiple_of(n * 32, 32), 32), :],
            send_sem=s1.at[to], recv_sem=r1.at[n],
            device_id=(blk, to), device_id_type=MESH,
        )

    for step, other in NARROW:
        send1(nar, narrow_peer(step, other)).start()

    def send_list(step, other):
        slot = step * 2 + other
        return pltpu.make_async_remote_copy(
            src_ref=lists.at[0], dst_ref=lists_v.at[slot],
            send_sem=sl.at[slot], recv_sem=rl.at[slot],
            device_id=(yh * 8 + row_peer(4 - step, other), nar), device_id_type=MESH,
        )

    for step, other in ROW:
        send_list(step, other).start()
    get_t.start()
    get_hw.start()

    get_w.wait()
    get_deg.wait()
    wh, wl = split(w_v[...].T)
    inv = lax.rsqrt(deg_v[pl.ds(pl.multiple_of(nar * 8, 8), 8), :].astype(jnp.float32))
    get_own.wait()
    for step, other in NARROW:
        n = narrow_peer(step, other)
        send1(n, n).wait_recv()

    for b in range(8):
        xh, xl = split(xt[:, b * TILE : (b + 1) * TILE])
        y = nn_dot(wh, xh) + nn_dot(wl, xh) + nn_dot(wh, xl)
        y = y * inv[b : b + 1, :]
        for n in range(8):
            for f in range(F):
                row = n * 32 + f * 8
                ysend[f, n, b] = y[row : row + 8, :]

    def send2(f, n, to):
        return pltpu.make_async_remote_copy(
            src_ref=ysend.at[f, to],
            dst_ref=y4[f].at[pl.ds(pl.multiple_of(n * 8, 8), 8)],
            send_sem=s2.at[f, to], recv_sem=r2.at[f, n],
            device_id=(blk, to), device_id_type=MESH,
        )

    def own2(f):
        return pltpu.make_async_copy(
            ysend.at[f, nar], y4[f].at[pl.ds(pl.multiple_of(nar * 8, 8), 8)], loc.at[6 + f]
        )

    for f in range(F):
        for step, other in NARROW:
            send2(f, nar, narrow_peer(step, other)).start()
        own2(f).start()

    get_list.wait()
    for step, other in ROW:
        send_list(step, other).wait_recv()
    to_smem = pltpu.make_async_copy(lists_v, lists_s, loc.at[10])
    to_smem.start()
    to_smem.wait()

    def send_y(f):
        return pltpu.make_async_remote_copy(
            src_ref=y4[f], dst_ref=yp[f], send_sem=sy.at[f], recv_sem=ry.at[f],
            device_id=(partner, nar), device_id_type=MESH,
        )

    def send_blocks(buf, got, ssem, rsem, part, source, step, other):
        slot = step * 2 + other
        return pltpu.make_async_remote_copy(
            src_ref=buf.at[part, slot], dst_ref=got.at[part, source],
            send_sem=ssem.at[part, slot], recv_sem=rsem.at[part, source],
            device_id=(yh * 8 + row_peer(step, other), nar), device_id_type=MESH,
        )

    def column(slot, source, k):
        return lists_s[slot, source, 1, k]

    def send_own(f, source, step, other):
        return send_blocks(own_b, got_own, so, ro, f, source, step, other)

    def send_early(f, source, step, other):
        return send_blocks(early_b, got_early, se, re, f, source, step, other)

    def send_late(q, source, step, other):
        return send_blocks(late_b, got_late, sq, rq, q, source, step, other)

    for f in range(F):
        own2(f).wait()
        for step, other in NARROW:
            n = narrow_peer(step, other)
            send2(f, n, n).wait_recv()
        send_y(f).start()
        for step, other in ROW:
            slot = step * 2 + other
            for k in range(SLOTS):
                own_b[f, slot, k] = y4[f][column(slot, blk, k)]
            send_own(f, me, step, other).start()
        for k in range(SLOTS):
            got_own[f, me, k] = y4[f][column(0, blk, k)]

    lane = lax.broadcasted_iota(jnp.int32, (8, TILE), 1)
    hub = jnp.zeros((8, TILE), jnp.float32)
    for h in range(8):
        node = hubs[0, h]
        here = lane == lax.rem(node, TILE)
        for f in range(F):
            col = jnp.sum(jnp.where(here, y4[f][node // TILE], 0.0), axis=1, keepdims=True)
            hub = jnp.where(lane == f * 8 + h, col, hub)
    hub_v[...] = hub
    hub_in[blk] = hub

    def swap_hub(source):
        return pltpu.make_async_remote_copy(
            src_ref=hub_v, dst_ref=hub_in.at[source], send_sem=sh.at[16], recv_sem=rh.at[source],
            device_id=(partner, nar), device_id_type=MESH,
        )

    def send_hub(src, source, sem, step, other):
        return pltpu.make_async_remote_copy(
            src_ref=src, dst_ref=hub_in.at[source], send_sem=sh.at[sem],
            recv_sem=rh.at[source],
            device_id=(yh * 8 + row_peer(step, other), nar), device_id_type=MESH,
        )

    swap_hub(blk).start()
    for step, other in ROW:
        send_hub(hub_v, blk, step * 2 + other, step, other).start()

    for f in range(2):
        send_y(f).wait_recv()
        for step, other in ROW:
            slot = step * 2 + other
            for k in range(SLOTS):
                early_b[f, slot, k] = yp[f][column(slot, partner, k)]
            send_early(f, me, step, other).start()
        for k in range(SLOTS):
            got_early[f, me, k] = yp[f][column(0, partner, k)]

    swap_hub(partner).wait_recv()
    for step, other in ROW:
        send_hub(hub_in.at[partner], partner, 8 + step * 2 + other, step, other).start()

    for f in range(2, F):
        send_y(f).wait_recv()
    for q in range(4):
        for step, other in ROW:
            slot = step * 2 + other
            for k in range(4):
                c = column(slot, partner, q * 4 + k)
                for f in range(2):
                    late_b[q, slot, f, k] = yp[2 + f][c]
            send_late(q, me, step, other).start()
        for k in range(4):
            c = column(0, partner, q * 4 + k)
            for f in range(2):
                got_late[q, me, f, k] = yp[2 + f][c]

    for step, other in ROW:
        peer = row_peer(step, other)
        for o in (yh * 8 + peer, (1 - yh) * 8 + peer):
            send_hub(hub_v, o, 0, step, other).wait_recv()
    parts = []
    for f in range(F):
        total = jnp.zeros((8, TILE), jnp.float32)
        for o in range(16):
            moved = pltpu.roll(hub_in[o], (o * 8 - f * 8) % TILE, 1)
            total = jnp.where(lane // 8 == o, moved, total)
        parts.append(total)
    gh, gl = split(jnp.concatenate(parts, axis=0))
    g2 = jnp.concatenate([gh, gl], axis=0)
    get_hw.wait()

    def hub_sum(i, carry):
        hh, hl = split(hw_v[:, pl.ds(pl.multiple_of(i * 512, 512), 512)])
        p = nn_dot(g2, hh)
        p = p[:32] + p[32:] + nn_dot(gh, hl)
        for b in range(4):
            for f in range(F):
                base[i * 4 + b, f] = (
                    p[f * 8 : f * 8 + 8, b * TILE : (b + 1) * TILE] + y4[f][i * 4 + b]
                )
        return carry

    lax.fori_loop(0, 16, hub_sum, 0)
    put_base = pltpu.make_async_copy(base, base_out, loc.at[16])
    put_base.start()

    get_t.wait()

    def product(xs, t):
        xh, xl = split(xs)
        th, tl = split(t_v[t])
        p = nt_dot(jnp.concatenate([xh, xl], axis=0), th)
        return p[:32] + p[32:] + nt_dot(xh, tl)

    for f in range(F):
        for step, other in ROW:
            send_own(f, row_peer(step, other), step, other).wait()

    def own_products(i, carry):
        for k in range(SLOTS):
            xs = jnp.concatenate([got_own[f, i, k] for f in range(F)], axis=0)
            p = product(xs, my_list[0, yh * 8 + i, 2, k])
            for f in range(F):
                p_own[i, k, f] = p[f * 8 : f * 8 + 8, :]
        return carry

    lax.fori_loop(0, 8, own_products, 0)
    put_own = pltpu.make_async_copy(p_own, prod_own, loc.at[11])
    put_own.start()

    for f in range(F):
        send_y(f).wait_send()
        for step, other in NARROW:
            n = narrow_peer(step, other)
            send2(f, n, n).wait_send()
    for step, other in NARROW:
        n = narrow_peer(step, other)
        send1(n, n).wait_send()
    for step, other in ROW:
        send_list(step, other).wait_send()
    swap_hub(partner).wait_send()
    for step, other in ROW:
        send_hub(hub_v, blk, step * 2 + other, step, other).wait_send()
        send_hub(hub_v, blk, 8 + step * 2 + other, step, other).wait_send()
    for f in range(2):
        for step, other in ROW:
            send_early(f, row_peer(step, other), step, other).wait()

    def put_par(q):
        return pltpu.make_async_copy(p_par.at[q], prod_par.at[q], loc.at[12 + q])

    for q in range(4):
        for step, other in ROW:
            send_late(q, row_peer(step, other), step, other).wait()

        def par_products(i, carry):
            for j in range(2):
                for k in range(4):
                    xs = jnp.concatenate(
                        [got_early[f, i * 2 + j, q * 4 + k] for f in range(2)]
                        + [got_late[q, i * 2 + j, f, k] for f in range(2)],
                        axis=0,
                    )
                    t = my_list[0, (1 - yh) * 8 + i * 2 + j, 2, q * 4 + k]
                    p = product(xs, t)
                    for f in range(F):
                        p_par[q, i * 2 + j, k, f] = p[f * 8 : f * 8 + 8, :]
            return carry

        lax.fori_loop(0, 4, par_products, 0)
        put_par(q).start()

    put_own.wait()
    put_base.wait()
    for q in range(4):
        put_par(q).wait()


def exchange(feat, deg, weight, lists, hubs, tiles, hub_w):
    f32 = jnp.float32
    dma = pltpu.SemaphoreType.DMA
    vmem = pltpu.VMEM
    smem = pl.BlockSpec(memory_space=pltpu.SMEM)
    hbm = pl.BlockSpec(memory_space=pl.ANY)
    tile = (8, TILE)
    return pl.pallas_call(
        exchange_kernel,
        out_shape=(
            jax.ShapeDtypeStruct((8, SLOTS, F, *tile), f32),
            jax.ShapeDtypeStruct((4, 8, 4, F, *tile), f32),
            jax.ShapeDtypeStruct((BLOCKS, F, *tile), f32),
        ),
        in_specs=[hbm, hbm, hbm, hbm, smem, smem, hbm, hbm],
        out_specs=(hbm, hbm, hbm),
        scratch_shapes=[
            vmem((256, 1024), f32),
            vmem((F, 8, 8, *tile), f32),
            *[vmem((BLOCKS, *tile), f32)] * 8,
            vmem((F, 8, SLOTS, *tile), f32),
            vmem((2, 8, SLOTS, *tile), f32),
            vmem((4, 8, 2, 4, *tile), f32),
            vmem((F, 8, SLOTS, *tile), f32),
            vmem((2, 8, SLOTS, *tile), f32),
            vmem((4, 8, 2, 4, *tile), f32),
            vmem((8, 16, 3, SLOTS), jnp.int32),
            pltpu.SMEM((8, 16, 3, SLOTS), jnp.int32),
            vmem(tile, f32),
            vmem((16, *tile), f32),
            vmem((BLOCKS, TILE), jnp.int32),
            vmem((256, 256), f32),
            vmem((TV, TILE, TILE), f32),
            vmem((128, BLOCKS * TILE), f32),
            vmem((8, SLOTS, F, *tile), f32),
            vmem((4, 8, 4, F, *tile), f32),
            vmem((BLOCKS, F, *tile), f32),
            dma((8,)), dma((8,)),
            dma((F, 8)), dma((F, 8)),
            dma((F,)), dma((F,)),
            dma((8,)), dma((8,)),
            dma((17,)), dma((16,)),
            dma((F, 8)), dma((F, 8)),
            dma((2, 8)), dma((2, 8)),
            dma((4, 8)), dma((4, 8)),
            dma((17,)),
        ],
        compiler_params=pltpu.CompilerParams(
            collective_id=0, has_side_effects=True, vmem_limit_bytes=56 * 2**20
        ),
    )(feat, deg, weight, lists, lists, hubs, tiles, hub_w)


def add_kernel(
    prod_own, prod_par, base, deg, bias, lists, counts,
    out,
    own_v, par_v, acc, deg_v, sem,
):
    get_base = pltpu.make_async_copy(base, acc, sem.at[0])
    get_own = pltpu.make_async_copy(prod_own, own_v, sem.at[1])
    get_par = pltpu.make_async_copy(prod_par, par_v, sem.at[2])
    get_deg = pltpu.make_async_copy(deg, deg_v, sem.at[3])
    copies = (get_base, get_own, get_par, get_deg)
    for copy in copies:
        copy.start()
    yh = lax.axis_index("blk") // 8
    nar = lax.axis_index("narrow")
    sub = lax.broadcasted_iota(jnp.int32, (8, TILE), 0)
    biases = []
    for f in range(F):
        column = jnp.zeros((8, TILE), jnp.float32)
        for i in range(8):
            column = jnp.where(sub == i, bias[nar * 32 + f * 8 + i], column)
        biases.append(column)
    for copy in copies:
        copy.wait()

    def own_source(i, carry):
        o = yh * 8 + i

        def slot(k, carry):
            r = lists[0, o, 0, k]
            acc[r] += own_v[i, k]
            return carry

        return lax.fori_loop(0, counts[0, o], slot, carry)

    def par_source(i, carry):
        o = (1 - yh) * 8 + i

        def slot(k, carry):
            r = lists[0, o, 0, k]
            acc[r] += par_v[k // 4, i, lax.rem(k, 4)]
            return carry

        return lax.fori_loop(0, counts[0, o], slot, carry)

    lax.fori_loop(0, 8, own_source, 0)
    lax.fori_loop(0, 8, par_source, 0)

    def finish(i, carry):
        inv = lax.rsqrt(deg_v[pl.ds(pl.multiple_of(i * 8, 8), 8), :].astype(jnp.float32))
        for b in range(8):
            for f in range(F):
                value = acc[i * 8 + b, f] * inv[b : b + 1, :] + biases[f]
                out[f * 8 : f * 8 + 8, pl.ds(pl.multiple_of((i * 8 + b) * TILE, TILE), TILE)] = (
                    jnp.maximum(value, 0.0)
                )
        return carry

    lax.fori_loop(0, 8, finish, 0)


def add_rows(prod_own, prod_par, base, deg, bias, lists, counts):
    f32 = jnp.float32
    vmem = pltpu.VMEM
    smem = pl.BlockSpec(memory_space=pltpu.SMEM)
    hbm = pl.BlockSpec(memory_space=pl.ANY)
    tile = (8, TILE)
    return pl.pallas_call(
        add_kernel,
        out_shape=jax.ShapeDtypeStruct((32, BLOCKS * TILE), f32),
        in_specs=[hbm, hbm, hbm, hbm, smem, smem, smem],
        out_specs=pl.BlockSpec(memory_space=vmem),
        scratch_shapes=[
            vmem((8, SLOTS, F, *tile), f32),
            vmem((4, 8, 4, F, *tile), f32),
            vmem((BLOCKS, F, *tile), f32),
            vmem((BLOCKS, TILE), jnp.int32),
            pltpu.SemaphoreType.DMA((4,)),
        ],
        compiler_params=pltpu.CompilerParams(vmem_limit_bytes=24 * 2**20),
    )(prod_own, prod_par, base, deg, bias, lists, counts)


def body(
    features, degrees, tile_values, tile_list, tile_count, hub_local, hub_weights, weight, out_bias
):
    deg = degrees.reshape(BLOCKS, TILE)
    own, par, base = exchange(
        features, deg, weight, tile_list, hub_local, tile_values, hub_weights
    )
    return add_rows(own, par, base, deg, out_bias, tile_list, tile_count)


def solution(mesh):
    return jax.shard_map(
        body,
        mesh=mesh,
        in_specs=(
            P("narrow", "blk"),
            P("blk"),
            P("blk", None, None),
            P("blk", None, None, None),
            P("blk", None),
            P("blk", None),
            P(None, "blk"),
            P(),
            P(),
        ),
        out_specs=P("narrow", "blk"),
        check_vma=False,
    )
```

time: 103 us -> 97.5 us (0.947)
  Pallas kernels: 95 us -> 90.9 us
  local copies, waits for them, and re-layouts: 7.37 us -> 5.78 us
    pallas_call x2, Pallas kernels: 95 us -> 90.9 us  [the longest x1 86.4 us: exchange(): pl.pallas_call(exchange_kernel, out_shape=(jax.ShapeDtypeStruct((8, SLOTS...]
    unnamed x13 -> x15, local copies, waits for them, and re-layouts: 5.74 us -> 5.78 us
where the time goes in v2:
time: 97.5 us; the launch traced here: 96.8 us
  Pallas kernels  90.9 us (93%)
  local copies, waits for them, and re-layouts  5.78 us (6%)
    pallas_call x1, Pallas kernels, exchange(): pl.pallas_call(exchange_kernel, out_shape=(jax.ShapeDtypeStruct((8, SLOTS...  86.4 us
    unnamed x15, local copies, waits for them, and re-layouts  5.78 us
    pallas_call x1, Pallas kernels, add_rows(): pl.pallas_call(add_kernel, out_shape=jax.ShapeDtypeStruct((32, BLOCKS * T...  4.55 us

profile of v2, /device:TPU:1, one launch (start us, length us, event | category | flops | bytes accessed | tf_op | source)
XLA Modules:
  0.0 96.8 jit_solution(4497061718625231983)
XLA Ops:
  0.0 1.4 %copy.10.lists.my_list = s32[1,16,3,16]{3,2,1,0:T(4,128)} copy(s32[1,16,3,16]{3,1,2,0:T(8,128)} %param.12) | data formatting | bytes 6144 | tf_op args[3]
  1.4 0.0 copy-start.3
  1.4 0.0 copy-start.4
  1.4 0.0 copy-start.5
  1.4 0.0 copy-start.6
  1.4 86.4 %shard_map.91 = (f32[8,16,4,8,128]{4,3,2,1,0:T(8,128)}, f32[4,8,4,4,8,128]{5,4,3,2,1,0:T(8,128)}, f32[64,4,8,128]{3,2,1,0:T(8,128)}) custom-call(f32[32,8192]{1,0:T(8,128)} %feat.1, s32[64,128]{1,0:T(8,128)} %bitcast.1, f32[256,256]{1,0:T(8,128)} %weight.1, s32[1,16,3,16]{3,2,1,0:T(4,128)} %copy.10.lists.my_list, s32[1,16,3,16]{3,2,1,0:T(4,128)} %copy.10.lists.my_list, ...), custom_call_target="tpu_custom_call" | custom-call | tf_op jit(solution)/shard_map/pallas_call | solution.py:353
  87.8 0.0 copy-done.3
  87.8 0.0 copy-done.4
  87.8 0.0 copy-done.5
  87.8 0.0 copy-done.6
  87.8 0.0 copy-start
  87.8 1.6 %copy-done = f32[8,16,4,8,128]{4,3,2,1,0:T(8,128)S(1)} copy-done((f32[8,16,4,8,128]{4,3,2,1,0:T(8,128)S(1)}, f32[8,16,4,8,128]{4,3,2,1,0:T(8,128)}, u32[]{:S(2)}) %copy-start) | copy-done | bytes 2097176
  89.4 0.0 copy-start.1
  89.4 1.6 %copy-done.1 = f32[4,8,4,4,8,128]{5,4,3,2,1,0:T(8,128)S(1)} copy-done((f32[4,8,4,4,8,128]{5,4,3,2,1,0:T(8,128)S(1)}, f32[4,8,4,4,8,128]{5,4,3,2,1,0:T(8,128)}, u32[]{:S(2)}) %copy-start.1) | copy-done | bytes 2097176
  91.0 0.0 copy-start.2
  91.0 1.2 %copy-done.2 = f32[64,4,8,128]{3,2,1,0:T(8,128)S(1)} copy-done((f32[64,4,8,128]{3,2,1,0:T(8,128)S(1)}, f32[64,4,8,128]{3,2,1,0:T(8,128)}, u32[]{:S(2)}) %copy-start.2) | copy-done | bytes 1048600
  92.2 4.5 %shard_map.92 = f32[32,8192]{1,0:T(8,128)} custom-call(f32[8,16,4,8,128]{4,3,2,1,0:T(8,128)S(1)} %copy-done, f32[4,8,4,4,8,128]{5,4,3,2,1,0:T(8,128)S(1)} %copy-done.1, f32[64,4,8,128]{3,2,1,0:T(8,128)S(1)} %copy-done.2, s32[64,128]{1,0:T(8,128)S(1)} %bitcast.2, f32[256]{0:T(256)S(1)} %copy-done.5, s32[1,16,3,16]{3,2,1,0:T(4,128)S(1)} %copy-done.3, ...), custom_call_target="tpu_custom_call" | custom-call | tf_op jit(solution)/shard_map/pallas_call | solution.py:465
Async XLA Ops:
  1.4 86.4 %copy-start.3 = (s32[1,16,3,16]{3,2,1,0:T(4,128)S(1)}, s32[1,16,3,16]{3,2,1,0:T(4,128)}, u32[]{:S(2)}) copy-start(s32[1,16,3,16]{3,2,1,0:T(4,128)} %copy.10.lists.my_list) | copy-start | bytes 9220
  1.4 86.4 %copy-start.4 = (s32[8192]{0:T(1024)S(1)}, s32[8192]{0:T(1024)}, u32[]{:S(2)}) copy-start(s32[8192]{0:T(1024)} %param.10) | copy-start | bytes 98308
  1.4 86.4 %copy-start.5 = (f32[256]{0:T(256)S(1)}, f32[256]{0:T(256)}, u32[]{:S(2)}) copy-start(f32[256]{0:T(256)} %bias.1) | copy-start | bytes 3076
  1.4 86.4 %copy-start.6 = (s32[1,16]{1,0:T(1,128)S(1)}, s32[1,16]{1,0:T(1,128)}, u32[]{:S(2)}) copy-start(s32[1,16]{1,0:T(1,128)} %counts.1) | copy-start | bytes 196
  87.8 1.6 %copy-start = (f32[8,16,4,8,128]{4,3,2,1,0:T(8,128)S(1)}, f32[8,16,4,8,128]{4,3,2,1,0:T(8,128)}, u32[]{:S(2)}) copy-start(f32[8,16,4,8,128]{4,3,2,1,0:T(8,128)} %get-tuple-element.8.prod_own) | copy-start | bytes 6291460
  89.4 1.6 %copy-start.1 = (f32[4,8,4,4,8,128]{5,4,3,2,1,0:T(8,128)S(1)}, f32[4,8,4,4,8,128]{5,4,3,2,1,0:T(8,128)}, u32[]{:S(2)}) copy-start(f32[4,8,4,4,8,128]{5,4,3,2,1,0:T(8,128)} %get-tuple-element.9.prod_par) | copy-start | bytes 6291460
  91.0 1.2 %copy-start.2 = (f32[64,4,8,128]{3,2,1,0:T(8,128)S(1)}, f32[64,4,8,128]{3,2,1,0:T(8,128)}, u32[]{:S(2)}) copy-start(f32[64,4,8,128]{3,2,1,0:T(8,128)} %get-tuple-element.10.base) | copy-start | bytes 3145732

commit v3 on v2

v3 whole, which is shorter than its diff:
```python
import functools

import jax
import jax.numpy as jnp
from jax import lax
from jax.experimental import pallas as pl
from jax.experimental.pallas import tpu as pltpu
from jax.sharding import PartitionSpec as P

TILE = 128
SLOTS = 16
F = 4
BLOCKS = 64
TV = 256
MESH = pl.DeviceIdType.MESH
ROW = ((1, 0), (3, 0), (1, 1), (3, 1), (2, 0), (2, 1), (0, 1))
NARROW = ((1, 0), (3, 0), (0, 1), (2, 0), (1, 1), (3, 1), (2, 1))


def split(x):
    hi = x.astype(jnp.bfloat16)
    lo = (x - hi.astype(jnp.float32)).astype(jnp.bfloat16)
    return hi, lo


def nt_dot(a, b):
    return lax.dot_general(a, b, (((1,), (1,)), ((), ())), preferred_element_type=jnp.float32)


def nn_dot(a, b):
    return jnp.dot(a, b, preferred_element_type=jnp.float32)


def exchange_kernel(
    feat, deg, weight, lists, my_list, counts, hubs, tiles, hub_w,
    out,
    xt, ysend, ya, yb, yc, yd, pa, pb, pc, pd, own_b, early_b, late_b,
    got_own, got_early, got_late, lists_v, lists_s, hub_v, hub_in, deg_v, w_v, raw_t, t_v, hw_v,
    order_v, order_s, value,
    s1, r1, s2, r2, sy, ry, sl, rl, sh, rh, so, ro, se, re, sq, rq, loc,
):
    y4, yp = (ya, yb, yc, yd), (pa, pb, pc, pd)
    blk = lax.axis_index("blk")
    nar = lax.axis_index("narrow")
    yh, x, core = blk // 8, (blk // 2) % 4, blk % 2
    z, yl = nar // 2, nar % 2
    me = x * 2 + core
    partner = (1 - yh) * 8 + me

    def row_peer(step, other):
        return lax.rem(x + step, 4) * 2 + lax.rem(core + other, 2)

    def narrow_peer(step, other):
        return lax.rem(z + step, 4) * 2 + lax.rem(yl + other, 2)

    bar = pltpu.get_barrier_semaphore()
    for step, other in NARROW:
        pl.semaphore_signal(
            bar, inc=1, device_id=(blk, narrow_peer(step, other)), device_id_type=MESH
        )
    for step, other in ROW:
        pl.semaphore_signal(
            bar, inc=1, device_id=(yh * 8 + row_peer(step, other), nar), device_id_type=MESH
        )
    pl.semaphore_signal(bar, inc=1, device_id=(partner, nar), device_id_type=MESH)

    get_deg = pltpu.make_async_copy(deg, deg_v, loc.at[0])
    get_w = pltpu.make_async_copy(weight, w_v, loc.at[1])
    get_own = pltpu.make_async_copy(
        feat.at[:, pl.ds(pl.multiple_of(nar * 1024, 1024), 1024)],
        xt.at[pl.ds(pl.multiple_of(nar * 32, 32), 32), :], loc.at[2],
    )
    get_list = pltpu.make_async_copy(lists.at[0, 1], lists_v.at[0], loc.at[3])
    def get_t(part):
        return pltpu.make_async_copy(
            tiles.at[pl.ds(part * 64, 64)], raw_t.at[part % 2], loc.at[11 + part]
        )

    get_hw = pltpu.make_async_copy(hub_w, hw_v, loc.at[5])
    for copy in (get_w, get_deg, get_own, get_list):
        copy.start()
    pl.semaphore_wait(bar, 15)

    def send1(n, to):
        return pltpu.make_async_remote_copy(
            src_ref=feat.at[:, pl.ds(pl.multiple_of(to * 1024, 1024), 1024)],
            dst_ref=xt.at[pl.ds(pl.multiple_of(n * 32, 32), 32), :],
            send_sem=s1.at[to], recv_sem=r1.at[n],
            device_id=(blk, to), device_id_type=MESH,
        )

    for step, other in NARROW:
        send1(nar, narrow_peer(step, other)).start()

    def send_list(step, other):
        slot = step * 2 + other
        return pltpu.make_async_remote_copy(
            src_ref=lists.at[0, 1], dst_ref=lists_v.at[slot],
            send_sem=sl.at[slot], recv_sem=rl.at[slot],
            device_id=(yh * 8 + row_peer(4 - step, other), nar), device_id_type=MESH,
        )

    for step, other in ROW:
        send_list(step, other).start()
    get_t(0).start()
    get_t(1).start()
    get_hw.start()

    get_w.wait()
    get_deg.wait()
    wh, wl = split(w_v[...].T)
    inv = lax.rsqrt(deg_v[pl.ds(pl.multiple_of(nar * 8, 8), 8), :].astype(jnp.float32))

    position = lax.broadcasted_iota(jnp.int32, (8, TILE), 0) * TILE + lax.broadcasted_iota(
        jnp.int32, (8, TILE), 1
    )

    def slot_at(s):
        late = s - 128
        own = s < 128
        i = jnp.where(own, s // 16, late % 32 // 4)
        k = jnp.where(own, s % 16, late // 32 * 4 + late % 4)
        o = jnp.where(own, yh, 1 - yh) * 8 + i
        return my_list[0, 0, o, k], k < counts[0, o]

    def fill(s, rows):
        r, live = slot_at(s)
        return jnp.where(position == s, jnp.where(live, r, 2000 + r), rows)

    rows = lax.fori_loop(0, TV, fill, jnp.zeros((8, TILE), jnp.int32))

    def link(s, carry):
        before, last = carry
        r, live = slot_at(s)
        r = jnp.where(live, r, 1000)
        before = jnp.where((rows == r) & (position > s), BLOCKS + s, before)
        return before, jnp.where(position == r, BLOCKS + s, last)

    before, last = lax.fori_loop(0, TV, link, (jnp.where(rows >= 2000, 0, rows), position))
    order_v[:8] = before
    order_v[8:] = last
    order_to_smem = pltpu.make_async_copy(order_v, order_s, loc.at[15])
    order_to_smem.start()

    for part in range(4):
        get_t(part).wait()

        def halves(t, carry, part=part):
            hi, lo = split(raw_t[part % 2, t])
            t_v[part * 64 + t, :, :TILE] = hi
            t_v[part * 64 + t, :, TILE:] = lo
            return carry

        lax.fori_loop(0, 64, halves, 0)
        if part < 2:
            get_t(part + 2).start()
    order_to_smem.wait()

    get_own.wait()
    for step, other in NARROW:
        n = narrow_peer(step, other)
        send1(n, n).wait_recv()

    for b in range(8):
        xh, xl = split(xt[:, b * TILE : (b + 1) * TILE])
        y = nn_dot(wh, xh) + nn_dot(wl, xh) + nn_dot(wh, xl)
        y = y * inv[b : b + 1, :]
        for n in range(8):
            for f in range(F):
                row = n * 32 + f * 8
                ysend[f, n, b] = y[row : row + 8, :]

    def send2(f, n, to):
        return pltpu.make_async_remote_copy(
            src_ref=ysend.at[f, to],
            dst_ref=y4[f].at[pl.ds(pl.multiple_of(n * 8, 8), 8)],
            send_sem=s2.at[f, to], recv_sem=r2.at[f, n],
            device_id=(blk, to), device_id_type=MESH,
        )

    def own2(f):
        return pltpu.make_async_copy(
            ysend.at[f, nar], y4[f].at[pl.ds(pl.multiple_of(nar * 8, 8), 8)], loc.at[6 + f]
        )

    for f in range(F):
        for step, other in NARROW:
            send2(f, nar, narrow_peer(step, other)).start()
        own2(f).start()

    get_list.wait()
    for step, other in ROW:
        send_list(step, other).wait_recv()
    to_smem = pltpu.make_async_copy(lists_v, lists_s, loc.at[10])
    to_smem.start()
    to_smem.wait()

    def send_y(f):
        return pltpu.make_async_remote_copy(
            src_ref=y4[f], dst_ref=yp[f], send_sem=sy.at[f], recv_sem=ry.at[f],
            device_id=(partner, nar), device_id_type=MESH,
        )

    def send_blocks(buf, got, ssem, rsem, part, source, step, other):
        slot = step * 2 + other
        return pltpu.make_async_remote_copy(
            src_ref=buf.at[part, slot], dst_ref=got.at[part, source],
            send_sem=ssem.at[part, slot], recv_sem=rsem.at[part, source],
            device_id=(yh * 8 + row_peer(step, other), nar), device_id_type=MESH,
        )

    def column(slot, source, k):
        return lists_s[slot, source, k]

    def send_own(f, source, step, other):
        return send_blocks(own_b, got_own, so, ro, f, source, step, other)

    def send_early(f, source, step, other):
        return send_blocks(early_b, got_early, se, re, f, source, step, other)

    def send_late(q, source, step, other):
        return send_blocks(late_b, got_late, sq, rq, q, source, step, other)

    for f in range(F):
        own2(f).wait()
        for step, other in NARROW:
            n = narrow_peer(step, other)
            send2(f, n, n).wait_recv()
        send_y(f).start()
        for step, other in ROW:
            slot = step * 2 + other
            for k in range(SLOTS):
                own_b[f, slot, k] = y4[f][column(slot, blk, k)]
            send_own(f, me, step, other).start()
        for k in range(SLOTS):
            got_own[f, me, k] = y4[f][column(0, blk, k)]

    lane = lax.broadcasted_iota(jnp.int32, (8, TILE), 1)
    hub = jnp.zeros((8, TILE), jnp.float32)
    for h in range(8):
        node = hubs[0, h]
        here = lane == lax.rem(node, TILE)
        for f in range(F):
            col = jnp.sum(jnp.where(here, y4[f][node // TILE], 0.0), axis=1, keepdims=True)
            hub = jnp.where(lane == f * 8 + h, col, hub)
    hub_v[...] = hub
    hub_in[blk] = hub

    def swap_hub(source):
        return pltpu.make_async_remote_copy(
            src_ref=hub_v, dst_ref=hub_in.at[source], send_sem=sh.at[16], recv_sem=rh.at[source],
            device_id=(partner, nar), device_id_type=MESH,
        )

    def send_hub(src, source, sem, step, other):
        return pltpu.make_async_remote_copy(
            src_ref=src, dst_ref=hub_in.at[source], send_sem=sh.at[sem],
            recv_sem=rh.at[source],
            device_id=(yh * 8 + row_peer(step, other), nar), device_id_type=MESH,
        )

    swap_hub(blk).start()
    for step, other in ROW:
        send_hub(hub_v, blk, step * 2 + other, step, other).start()

    def own_left(f):
        for step, other in ROW:
            send_own(f, me, step, other).wait_send()

    for f in range(2):
        send_y(f).wait_recv()
        own_left(f)
        for step, other in ROW:
            slot = step * 2 + other
            for k in range(SLOTS):
                early_b[f, slot, k] = yp[f][column(slot, partner, k)]
            send_early(f, me, step, other).start()
        for k in range(SLOTS):
            got_early[f, me, k] = yp[f][column(0, partner, k)]

    swap_hub(partner).wait_recv()
    for step, other in ROW:
        send_hub(hub_in.at[partner], partner, 8 + step * 2 + other, step, other).start()

    own_left(2)
    own_left(3)
    for f in range(F):
        send_y(f).wait_send()
        for step, other in NARROW:
            n = narrow_peer(step, other)
            send2(f, n, n).wait_send()
    for step, other in NARROW:
        n = narrow_peer(step, other)
        send1(n, n).wait_send()
    for step, other in ROW:
        send_list(step, other).wait_send()

    for step, other in ROW:
        peer = row_peer(step, other)
        for o in (yh * 8 + peer, (1 - yh) * 8 + peer):
            send_hub(hub_v, o, 0, step, other).wait_recv()
    parts = []
    for f in range(F):
        total = jnp.zeros((8, TILE), jnp.float32)
        for o in range(16):
            moved = pltpu.roll(hub_in[o], (o * 8 - f * 8) % TILE, 1)
            total = jnp.where(lane // 8 == o, moved, total)
        parts.append(total)
    gh, gl = split(jnp.concatenate(parts, axis=0))
    g2 = jnp.concatenate([gh, gl], axis=0)
    get_hw.wait()

    def hub_sum(i, carry):
        hh, hl = split(hw_v[:, pl.ds(pl.multiple_of(i * 512, 512), 512)])
        p = nn_dot(g2, hh)
        p = p[:32] + p[32:] + nn_dot(gh, hl)
        for b in range(4):
            for f in range(F):
                value[i * 4 + b, f] = (
                    p[f * 8 : f * 8 + 8, b * TILE : (b + 1) * TILE] + y4[f][i * 4 + b]
                )
        return carry

    lax.fori_loop(0, 16, hub_sum, 0)

    def product(xs, t):
        xh, xl = split(xs)
        x2 = jnp.concatenate(
            [
                jnp.concatenate([xh, xh], axis=1),
                jnp.concatenate([xl, jnp.zeros_like(xl)], axis=1),
            ],
            axis=0,
        )
        p = nt_dot(x2, t_v[t])
        return p[:32] + p[32:]

    def add(products, first):
        for j, p in enumerate(products):
            s = first + j
            back = order_s[s // TILE, lax.rem(s, TILE)]
            for f in range(F):
                value[BLOCKS + s, f] = p[f * 8 : f * 8 + 8, :] + value[back, f]

    def own_products(i, carry):
        for half in range(2):
            products = []
            for k in range(half * 8, half * 8 + 8):
                xs = jnp.concatenate([got_own[f, i, k] for f in range(F)], axis=0)
                products.append(product(xs, my_list[0, 2, yh * 8 + i, k]))
            add(products, i * 16 + half * 8)
        return carry

    def par_products(q):
        def pair(i, carry):
            products = []
            for j in range(2):
                for k in range(4):
                    xs = jnp.concatenate(
                        [got_early[f, i * 2 + j, q * 4 + k] for f in range(2)]
                        + [got_late[q, i * 2 + j, f, k] for f in range(2)],
                        axis=0,
                    )
                    t = my_list[0, 2, (1 - yh) * 8 + i * 2 + j, q * 4 + k]
                    products.append(product(xs, t))
            add(products, 128 + q * 32 + i * 8)
            return carry

        lax.fori_loop(0, 4, pair, 0)

    for f in range(2, F):
        send_y(f).wait_recv()

    def start_late(q):
        for step, other in ROW:
            slot = step * 2 + other
            for k in range(4):
                c = column(slot, partner, q * 4 + k)
                for f in range(2):
                    late_b[q, slot, f, k] = yp[2 + f][c]
            send_late(q, me, step, other).start()
        for k in range(4):
            c = column(0, partner, q * 4 + k)
            for f in range(2):
                got_late[q, me, f, k] = yp[2 + f][c]

    def late_done(q):
        for step, other in ROW:
            send_late(q, row_peer(step, other), step, other).wait()

    start_late(0)
    start_late(1)
    for f in range(F):
        for step, other in ROW:
            send_own(f, row_peer(step, other), step, other).wait_recv()
    lax.fori_loop(0, 8, own_products, 0)
    swap_hub(partner).wait_send()
    for step, other in ROW:
        send_hub(hub_v, blk, step * 2 + other, step, other).wait_send()
        send_hub(hub_v, blk, 8 + step * 2 + other, step, other).wait_send()
    for f in range(2):
        for step, other in ROW:
            send_early(f, row_peer(step, other), step, other).wait()
    for q in range(4):
        late_done(q)
        if q < 2:
            start_late(q + 2)
        par_products(q)

    def finish(i, carry):
        inv = lax.rsqrt(deg_v[pl.ds(pl.multiple_of(i * 8, 8), 8), :].astype(jnp.float32))
        for b in range(8):
            end = order_s[8, i * 8 + b]
            for f in range(F):
                out[f * 8 : f * 8 + 8, pl.ds(pl.multiple_of((i * 8 + b) * TILE, TILE), TILE)] = (
                    value[end, f] * inv[b : b + 1, :]
                )
        return carry

    lax.fori_loop(0, 8, finish, 0)


def exchange(feat, deg, weight, lists, counts, hubs, tiles, hub_w):
    f32, bf16 = jnp.float32, jnp.bfloat16
    dma = pltpu.SemaphoreType.DMA
    vmem = pltpu.VMEM
    smem = pl.BlockSpec(memory_space=pltpu.SMEM)
    hbm = pl.BlockSpec(memory_space=pl.ANY)
    tile = (8, TILE)
    return pl.pallas_call(
        exchange_kernel,
        out_shape=jax.ShapeDtypeStruct((32, BLOCKS * TILE), f32),
        in_specs=[hbm, hbm, hbm, hbm, smem, smem, smem, hbm, hbm],
        out_specs=pl.BlockSpec(memory_space=vmem),
        scratch_shapes=[
            vmem((256, 1024), f32),
            vmem((F, 8, 8, *tile), f32),
            *[vmem((BLOCKS, *tile), f32)] * 8,
            vmem((F, 8, SLOTS, *tile), f32),
            vmem((2, 8, SLOTS, *tile), f32),
            vmem((4, 8, 2, 4, *tile), f32),
            vmem((F, 8, SLOTS, *tile), f32),
            vmem((2, 8, SLOTS, *tile), f32),
            vmem((4, 8, 2, 4, *tile), f32),
            vmem((8, 16, SLOTS), jnp.int32),
            pltpu.SMEM((8, 16, SLOTS), jnp.int32),
            vmem(tile, f32),
            vmem((16, *tile), f32),
            vmem((BLOCKS, TILE), jnp.int32),
            vmem((256, 256), f32),
            vmem((2, 64, TILE, TILE), f32),
            vmem((TV, TILE, 2 * TILE), bf16),
            vmem((128, BLOCKS * TILE), f32),
            vmem((16, TILE), jnp.int32),
            pltpu.SMEM((16, TILE), jnp.int32),
            vmem((BLOCKS + TV, F, *tile), f32),
            dma((8,)), dma((8,)),
            dma((F, 8)), dma((F, 8)),
            dma((F,)), dma((F,)),
            dma((8,)), dma((8,)),
            dma((17,)), dma((16,)),
            dma((F, 8)), dma((F, 8)),
            dma((2, 8)), dma((2, 8)),
            dma((4, 8)), dma((4, 8)),
            dma((16,)),
        ],
        compiler_params=pltpu.CompilerParams(
            collective_id=0, has_side_effects=True, vmem_limit_bytes=60 * 2**20
        ),
    )(feat, deg, weight, lists, lists, counts, hubs, tiles, hub_w)


def body(
    features, degrees, tile_values, tile_list, tile_count, hub_local, hub_weights, weight, out_bias
):
    deg = degrees.reshape(BLOCKS, TILE)
    lists = jnp.transpose(tile_list, (0, 2, 1, 3))
    aggregated = exchange(
        features, deg, weight, lists, tile_count, hub_local, tile_values, hub_weights
    )
    bias = lax.dynamic_slice_in_dim(out_bias, lax.axis_index("narrow") * 32, 32)
    return jnp.maximum(aggregated + bias[:, None], 0.0)


def solution(mesh):
    return jax.shard_map(
        body,
        mesh=mesh,
        in_specs=(
            P("narrow", "blk"),
            P("blk"),
            P("blk", None, None),
            P("blk", None, None, None),
            P("blk", None),
            P("blk", None),
            P(None, "blk"),
            P(),
            P(),
        ),
        out_specs=P("narrow", "blk"),
        check_vma=False,
    )
```

time: 97.5 us -> 96.7 us (level)
  local copies, waits for them, and re-layouts: 5.78 us -> 0.75 us
  Pallas kernels: 90.9 us -> 93.3 us
  other arithmetic: 0 us -> 2.34 us
    unnamed x15 -> x0, local copies, waits for them, and re-layouts: 5.78 us -> none
    pallas_call x2 -> x1, Pallas kernels: 90.9 us -> 93.3 us  [exchange(): pl.pallas_call(exchange_kernel, out_shape=jax.ShapeDtypeStruct((32, BLOCK...]
    max x0 -> x1, other arithmetic: none -> 2.34 us  [body(): return jnp.maximum(aggregated + bias[:, None], 0.0)]
where the time goes in v3:
time: 96.7 us; the launch traced here: 96.4 us
  Pallas kernels  93.3 us (96%)
  other arithmetic  2.34 us (2%)
    pallas_call x1, Pallas kernels, exchange(): pl.pallas_call(exchange_kernel, out_shape=jax.ShapeDtypeStruct((32, BLOCK...  93.3 us
    max x1, other arithmetic, body(): return jnp.maximum(aggregated + bias[:, None], 0.0)  2.34 us

profile of v3, /device:TPU:1, one launch (start us, length us, event | category | flops | bytes accessed | tf_op | source)
XLA Modules:
  0.0 96.4 jit_solution(8281706253501218345)
XLA Ops:
  0.0 0.8 dynamic_slice.3
  0.8 93.3 %shard_map.91 = f32[32,8192]{1,0:T(8,128)} custom-call(f32[32,8192]{1,0:T(8,128)} %feat.1, s32[64,128]{1,0:T(8,128)} %bitcast.4, f32[256,256]{1,0:T(8,128)} %weight.1, s32[1,3,16,16]{3,2,1,0:T(8,128)} %bitcast.2, s32[1,3,16,16]{3,2,1,0:T(8,128)} %bitcast.3, s32[1,16]{1,0:T(1,128)} %counts.1, s32[1,8]{1,0:T(1,128)} %hubs.1, f32[256,128,128]{2,1,0:T(8,128)} %tiles.1, ...), custom_call_target="tpu_custom_call" | custom-call | tf_op jit(solution)/shard_map/pallas_call | solution.py:430
  94.0 2.3 %add_maximum_fusion = f32[32,8192]{1,0:T(8,128)} fusion(f32[32,8192]{1,0:T(8,128)} %shard_map.91, f32[32]{0:T(128)S(1)} %dynamic_slice.3), kind=kLoop, calls=%fused_computation | loop fusion | flops 524288 | bytes 2097280 | tf_op jit(solution)/shard_map/max | solution.py:482

commit v4 on v3

--- a/solution.py
+++ b/solution.py
@@ -32,11 +32,11 @@
 
 
 def exchange_kernel(
-    feat, deg, weight, lists, my_list, counts, hubs, tiles, hub_w,
+    feat, deg, weight, lists, my_list, counts, hubs, bias, tiles, hub_w,
     out,
     xt, ysend, ya, yb, yc, yd, pa, pb, pc, pd, own_b, early_b, late_b,
     got_own, got_early, got_late, lists_v, lists_s, hub_v, hub_in, deg_v, w_v, raw_t, t_v, hw_v,
-    order_v, order_s, value,
+    order_v, order_s, value, hub_sums,
     s1, r1, s2, r2, sy, ry, sl, rl, sh, rh, so, ro, se, re, sq, rq, loc,
 ):
     y4, yp = (ya, yb, yc, yd), (pa, pb, pc, pd)
@@ -115,28 +115,44 @@
         jnp.int32, (8, TILE), 1
     )
 
-    def slot_at(s):
-        late = s - 128
-        own = s < 128
-        i = jnp.where(own, s // 16, late % 32 // 4)
-        k = jnp.where(own, s % 16, late // 32 * 4 + late % 4)
-        o = jnp.where(own, yh, 1 - yh) * 8 + i
-        return my_list[0, 0, o, k], k < counts[0, o]
-
-    def fill(s, rows):
-        r, live = slot_at(s)
-        return jnp.where(position == s, jnp.where(live, r, 2000 + r), rows)
-
-    rows = lax.fori_loop(0, TV, fill, jnp.zeros((8, TILE), jnp.int32))
-
-    def link(s, carry):
+    def key(o, k, dead):
+        r = my_list[0, 0, o, k]
+        return jnp.where(k < counts[0, o], r, dead + r)
+
+    def fill_own(i, rows):
+        for k in range(SLOTS):
+            rows = jnp.where(position == i * 16 + k, key(yh * 8 + i, k, 2000), rows)
+        return rows
+
+    def fill_par(i, rows):
+        for k in range(SLOTS):
+            s = 128 + k // 4 * 32 + i * 4 + k % 4
+            rows = jnp.where(position == s, key((1 - yh) * 8 + i, k, 2000), rows)
+        return rows
+
+    rows = lax.fori_loop(0, 8, fill_own, jnp.zeros((8, TILE), jnp.int32))
+    rows = lax.fori_loop(0, 8, fill_par, rows)
+
+    def link(r, s, carry):
         before, last = carry
-        r, live = slot_at(s)
-        r = jnp.where(live, r, 1000)
         before = jnp.where((rows == r) & (position > s), BLOCKS + s, before)
         return before, jnp.where(position == r, BLOCKS + s, last)
 
-    before, last = lax.fori_loop(0, TV, link, (jnp.where(rows >= 2000, 0, rows), position))
+    def link_own(i, carry):
+        for k in range(SLOTS):
+            carry = link(key(yh * 8 + i, k, 1000), i * 16 + k, carry)
+        return carry
+
+    def link_par(i, carry):
+        for k in range(SLOTS):
+            o = (1 - yh) * 8 + lax.rem(i, 2) * 4 + k // 4
+            s = 128 + i * 16 + k
+            carry = link(key(o, i // 2 * 4 + k % 4, 1000), s, carry)
+        return carry
+
+    carry = jnp.where(rows >= 2000, 0, rows), position
+    carry = lax.fori_loop(0, 8, link_own, carry)
+    before, last = lax.fori_loop(0, 8, link_par, carry)
     order_v[:8] = before
     order_v[8:] = last
     order_to_smem = pltpu.make_async_copy(order_v, order_s, loc.at[15])
@@ -221,11 +237,39 @@
     def send_late(q, source, step, other):
         return send_blocks(late_b, got_late, sq, rq, q, source, step, other)
 
+    lane = lax.broadcasted_iota(jnp.int32, (8, TILE), 1)
+
+    def swap_hub(source):
+        return pltpu.make_async_remote_copy(
+            src_ref=hub_v, dst_ref=hub_in.at[source], send_sem=sh.at[16], recv_sem=rh.at[source],
+            device_id=(partner, nar), device_id_type=MESH,
+        )
+
+    def send_hub(src, source, sem, step, other):
+        return pltpu.make_async_remote_copy(
+            src_ref=src, dst_ref=hub_in.at[source], send_sem=sh.at[sem],
+            recv_sem=rh.at[source],
+            device_id=(yh * 8 + row_peer(step, other), nar), device_id_type=MESH,
+        )
+
     for f in range(F):
         own2(f).wait()
         for step, other in NARROW:
             n = narrow_peer(step, other)
             send2(f, n, n).wait_recv()
+        if f == F - 1:
+            hub = jnp.zeros((8, TILE), jnp.float32)
+            for h in range(8):
+                node = hubs[0, h]
+                here = lane == lax.rem(node, TILE)
+                for g in range(F):
+                    col = jnp.sum(jnp.where(here, y4[g][node // TILE], 0.0), axis=1, keepdims=True)
+                    hub = jnp.where(lane == g * 8 + h, col, hub)
+            hub_v[...] = hub
+            hub_in[blk] = hub
+            swap_hub(blk).start()
+            for step, other in ROW:
+                send_hub(hub_v, blk, step * 2 + other, step, other).start()
         send_y(f).start()
         for step, other in ROW:
             slot = step * 2 + other
@@ -235,41 +279,13 @@
         for k in range(SLOTS):
             got_own[f, me, k] = y4[f][column(0, blk, k)]
 
-    lane = lax.broadcasted_iota(jnp.int32, (8, TILE), 1)
-    hub = jnp.zeros((8, TILE), jnp.float32)
-    for h in range(8):
-        node = hubs[0, h]
-        here = lane == lax.rem(node, TILE)
+    def keep_y(b, carry):
         for f in range(F):
-            col = jnp.sum(jnp.where(here, y4[f][node // TILE], 0.0), axis=1, keepdims=True)
-            hub = jnp.where(lane == f * 8 + h, col, hub)
-    hub_v[...] = hub
-    hub_in[blk] = hub
-
-    def swap_hub(source):
-        return pltpu.make_async_remote_copy(
-            src_ref=hub_v, dst_ref=hub_in.at[source], send_sem=sh.at[16], recv_sem=rh.at[source],
-            device_id=(partner, nar), device_id_type=MESH,
-        )
-
-    def send_hub(src, source, sem, step, other):
-        return pltpu.make_async_remote_copy(
-            src_ref=src, dst_ref=hub_in.at[source], send_sem=sh.at[sem],
-            recv_sem=rh.at[source],
-            device_id=(yh * 8 + row_peer(step, other), nar), device_id_type=MESH,
-        )
-
-    swap_hub(blk).start()
-    for step, other in ROW:
-        send_hub(hub_v, blk, step * 2 + other, step, other).start()
-
-    def own_left(f):
-        for step, other in ROW:
-            send_own(f, me, step, other).wait_send()
+            value[b, f] = y4[f][b]
+        return carry
 
     for f in range(2):
         send_y(f).wait_recv()
-        own_left(f)
         for step, other in ROW:
             slot = step * 2 + other
             for k in range(SLOTS):
@@ -278,50 +294,10 @@
         for k in range(SLOTS):
             got_early[f, me, k] = yp[f][column(0, partner, k)]
 
+    lax.fori_loop(0, BLOCKS, keep_y, 0)
     swap_hub(partner).wait_recv()
     for step, other in ROW:
         send_hub(hub_in.at[partner], partner, 8 + step * 2 + other, step, other).start()
-
-    own_left(2)
-    own_left(3)
-    for f in range(F):
-        send_y(f).wait_send()
-        for step, other in NARROW:
-            n = narrow_peer(step, other)
-            send2(f, n, n).wait_send()
-    for step, other in NARROW:
-        n = narrow_peer(step, other)
-        send1(n, n).wait_send()
-    for step, other in ROW:
-        send_list(step, other).wait_send()
-
-    for step, other in ROW:
-        peer = row_peer(step, other)
-        for o in (yh * 8 + peer, (1 - yh) * 8 + peer):
-            send_hub(hub_v, o, 0, step, other).wait_recv()
-    parts = []
-    for f in range(F):
-        total = jnp.zeros((8, TILE), jnp.float32)
-        for o in range(16):
-            moved = pltpu.roll(hub_in[o], (o * 8 - f * 8) % TILE, 1)
-            total = jnp.where(lane // 8 == o, moved, total)
-        parts.append(total)
-    gh, gl = split(jnp.concatenate(parts, axis=0))
-    g2 = jnp.concatenate([gh, gl], axis=0)
-    get_hw.wait()
-
-    def hub_sum(i, carry):
-        hh, hl = split(hw_v[:, pl.ds(pl.multiple_of(i * 512, 512), 512)])
-        p = nn_dot(g2, hh)
-        p = p[:32] + p[32:] + nn_dot(gh, hl)
-        for b in range(4):
-            for f in range(F):
-                value[i * 4 + b, f] = (
-                    p[f * 8 : f * 8 + 8, b * TILE : (b + 1) * TILE] + y4[f][i * 4 + b]
-                )
-        return carry
-
-    lax.fori_loop(0, 16, hub_sum, 0)
 
     def product(xs, t):
         xh, xl = split(xs)
@@ -388,12 +364,49 @@
         for step, other in ROW:
             send_late(q, row_peer(step, other), step, other).wait()
 
-    start_late(0)
-    start_late(1)
+    for q in range(4):
+        start_late(q)
     for f in range(F):
         for step, other in ROW:
-            send_own(f, row_peer(step, other), step, other).wait_recv()
+            send_own(f, row_peer(step, other), step, other).wait()
     lax.fori_loop(0, 8, own_products, 0)
+
+    for step, other in ROW:
+        peer = row_peer(step, other)
+        for o in (yh * 8 + peer, (1 - yh) * 8 + peer):
+            send_hub(hub_v, o, 0, step, other).wait_recv()
+    parts = []
+    for f in range(F):
+        total = jnp.zeros((8, TILE), jnp.float32)
+        for o in range(16):
+            moved = pltpu.roll(hub_in[o], (o * 8 - f * 8) % TILE, 1)
+            total = jnp.where(lane // 8 == o, moved, total)
+        parts.append(total)
+    gh, gl = split(jnp.concatenate(parts, axis=0))
+    g2 = jnp.concatenate([gh, gl], axis=0)
+    get_hw.wait()
+
+    def hub_sum(i, carry):
+        hh, hl = split(hw_v[:, pl.ds(pl.multiple_of(i * 512, 512), 512)])
+        p = nn_dot(g2, hh)
+        p = p[:32] + p[32:] + nn_dot(gh, hl)
+        for b in range(4):
+            for f in range(F):
+                hub_sums[i * 4 + b, f] = p[f * 8 : f * 8 + 8, b * TILE : (b + 1) * TILE]
+        return carry
+
+    lax.fori_loop(0, 16, hub_sum, 0)
+
+    for f in range(F):
+        send_y(f).wait_send()
+        for step, other in NARROW:
+            n = narrow_peer(step, other)
+            send2(f, n, n).wait_send()
+    for step, other in NARROW:
+        n = narrow_peer(step, other)
+        send1(n, n).wait_send()
+    for step, other in ROW:
+        send_list(step, other).wait_send()
     swap_hub(partner).wait_send()
     for step, other in ROW:
         send_hub(hub_v, blk, step * 2 + other, step, other).wait_send()
@@ -403,9 +416,15 @@
             send_early(f, row_peer(step, other), step, other).wait()
     for q in range(4):
         late_done(q)
-        if q < 2:
-            start_late(q + 2)
         par_products(q)
+
+    sub = lax.broadcasted_iota(jnp.int32, (8, TILE), 0)
+    biases = []
+    for f in range(F):
+        column_f = jnp.zeros((8, TILE), jnp.float32)
+        for i in range(8):
+            column_f = jnp.where(sub == i, bias[nar * 32 + f * 8 + i], column_f)
+        biases.append(column_f)
 
     def finish(i, carry):
         inv = lax.rsqrt(deg_v[pl.ds(pl.multiple_of(i * 8, 8), 8), :].astype(jnp.float32))
@@ -413,14 +432,17 @@
             end = order_s[8, i * 8 + b]
             for f in range(F):
                 out[f * 8 : f * 8 + 8, pl.ds(pl.multiple_of((i * 8 + b) * TILE, TILE), TILE)] = (
-                    value[end, f] * inv[b : b + 1, :]
+                    jnp.maximum(
+                        (value[end, f] + hub_sums[i * 8 + b, f]) * inv[b : b + 1, :] + biases[f],
+                        0.0,
+                    )
                 )
         return carry
 
     lax.fori_loop(0, 8, finish, 0)
 
 
-def exchange(feat, deg, weight, lists, counts, hubs, tiles, hub_w):
+def exchange(feat, deg, weight, lists, counts, hubs, bias, tiles, hub_w):
     f32, bf16 = jnp.float32, jnp.bfloat16
     dma = pltpu.SemaphoreType.DMA
     vmem = pltpu.VMEM
@@ -430,7 +452,7 @@
     return pl.pallas_call(
         exchange_kernel,
         out_shape=jax.ShapeDtypeStruct((32, BLOCKS * TILE), f32),
-        in_specs=[hbm, hbm, hbm, hbm, smem, smem, smem, hbm, hbm],
+        in_specs=[hbm, hbm, hbm, hbm, smem, smem, smem, smem, hbm, hbm],
         out_specs=pl.BlockSpec(memory_space=vmem),
         scratch_shapes=[
             vmem((256, 1024), f32),
@@ -454,6 +476,7 @@
             vmem((16, TILE), jnp.int32),
             pltpu.SMEM((16, TILE), jnp.int32),
             vmem((BLOCKS + TV, F, *tile), f32),
+            vmem((BLOCKS, F, *tile), f32),
             dma((8,)), dma((8,)),
             dma((F, 8)), dma((F, 8)),
             dma((F,)), dma((F,)),
@@ -467,7 +490,7 @@
         compiler_params=pltpu.CompilerParams(
             collective_id=0, has_side_effects=True, vmem_limit_bytes=60 * 2**20
         ),
-    )(feat, deg, weight, lists, lists, counts, hubs, tiles, hub_w)
+    )(feat, deg, weight, lists, lists, counts, hubs, bias, tiles, hub_w)
 
 
 def body(
@@ -475,11 +498,9 @@
 ):
     deg = degrees.reshape(BLOCKS, TILE)
     lists = jnp.transpose(tile_list, (0, 2, 1, 3))
-    aggregated = exchange(
-        features, deg, weight, lists, tile_count, hub_local, tile_values, hub_weights
+    return exchange(
+        features, deg, weight, lists, tile_count, hub_local, out_bias, tile_values, hub_weights
     )
-    bias = lax.dynamic_slice_in_dim(out_bias, lax.axis_index("narrow") * 32, 32)
-    return jnp.maximum(aggregated + bias[:, None], 0.0)
 
 
 def solution(mesh):

time: 96.7 us -> 83 us (0.86)
  Pallas kernels: 93.3 us -> 80.5 us
  other arithmetic: 2.34 us -> 0 us
  local copies, waits for them, and re-layouts: 0.75 us -> 2.26 us
    pallas_call x1, Pallas kernels: 93.3 us -> 80.5 us  [exchange(): pl.pallas_call(exchange_kernel, out_shape=jax.ShapeDtypeStruct((32, BLOCK...]
    max x1 -> x0, other arithmetic: 2.34 us -> none  [body(): return jnp.maximum(aggregated + bias[:, None], 0.0)]
    unnamed x0 -> x1, local copies, waits for them, and re-layouts: none -> 2.26 us
where the time goes in v4:
time: 83 us; the launch traced here: 82.7 us
  Pallas kernels  80.5 us (97%)
  local copies, waits for them, and re-layouts  2.26 us (3%)
    pallas_call x1, Pallas kernels, exchange(): pl.pallas_call(exchange_kernel, out_shape=jax.ShapeDtypeStruct((32, BLOCK...  80.5 us
    unnamed x1, local copies, waits for them, and re-layouts  2.26 us

profile of v4, /device:TPU:1, one launch (start us, length us, event | category | flops | bytes accessed | tf_op | source)
XLA Modules:
  0.0 82.7 jit_solution(17932874280894866703)
XLA Ops:
  0.0 80.5 %shard_map.91 = f32[32,8192]{1,0:T(8,128)} custom-call(f32[32,8192]{1,0:T(8,128)} %feat.1, s32[64,128]{1,0:T(8,128)} %bitcast.4, f32[256,256]{1,0:T(8,128)} %weight.1, s32[1,3,16,16]{3,2,1,0:T(8,128)} %bitcast.2, s32[1,3,16,16]{3,2,1,0:T(8,128)} %bitcast.3, s32[1,16]{1,0:T(1,128)} %counts.1, s32[1,8]{1,0:T(1,128)} %hubs.1, f32[256]{0:T(256)} %bias.1, ...), custom_call_target="tpu_custom_call" | custom-call | tf_op jit(solution)/shard_map/pallas_call | solution.py:452
  80.5 2.3 %copy.11 = f32[32,8192]{1,0:T(8,128)} copy(f32[32,8192]{1,0:T(8,128)} %shard_map.91) | data formatting | bytes 2097152

commit v5 on v4

--- a/solution.py
+++ b/solution.py
@@ -12,8 +12,10 @@
 F = 4
 BLOCKS = 64
 TV = 256
+LEVELS = ((0, 4), (4, 4), (8, 4), (12, 2), (14, 2))
 MESH = pl.DeviceIdType.MESH
-ROW = ((1, 0), (3, 0), (1, 1), (3, 1), (2, 0), (2, 1), (0, 1))
+ROW = ((2, 0), (2, 1), (1, 0), (3, 0), (1, 1), (3, 1), (0, 1))
+FAR = ((2, 1), (1, 1), (3, 1), (0, 1), (2, 0), (1, 0), (3, 0))
 NARROW = ((1, 0), (3, 0), (0, 1), (2, 0), (1, 1), (3, 1), (2, 1))
 
 
@@ -33,13 +35,14 @@
 
 def exchange_kernel(
     feat, deg, weight, lists, my_list, counts, hubs, bias, tiles, hub_w,
-    out,
-    xt, ysend, ya, yb, yc, yd, pa, pb, pc, pd, own_b, early_b, late_b,
+    out_hbm,
+    xt, ysend, ya, yb, yc, yd, pb, pc, pd, own_b, early_b, late_b,
+    row1, row2, row3, sel_b, got_first,
     got_own, got_early, got_late, lists_v, lists_s, hub_v, hub_in, deg_v, w_v, raw_t, t_v, hw_v,
-    order_v, order_s, value, hub_sums,
-    s1, r1, s2, r2, sy, ry, sl, rl, sh, rh, so, ro, se, re, sq, rq, loc,
+    order_v, order_s, value, hub_sums, out,
+    s1, r1, s2, r2, sy, ry, sl, rl, sh, rh, so, ro, se, re, sq, rq, sb, rb, sf, rf, loc,
 ):
-    y4, yp = (ya, yb, yc, yd), (pa, pb, pc, pd)
+    y4, yp = (ya, yb, yc, yd), (None, pb, pc, pd)
     blk = lax.axis_index("blk")
     nar = lax.axis_index("narrow")
     yh, x, core = blk // 8, (blk // 2) % 4, blk % 2
@@ -62,7 +65,9 @@
         pl.semaphore_signal(
             bar, inc=1, device_id=(yh * 8 + row_peer(step, other), nar), device_id_type=MESH
         )
-    pl.semaphore_signal(bar, inc=1, device_id=(partner, nar), device_id_type=MESH)
+    chip = (None, blk - core + 1 - core, partner, partner - core + 1 - core)
+    for to in chip[2:]:
+        pl.semaphore_signal(bar, inc=1, device_id=(to, nar), device_id_type=MESH)
 
     get_deg = pltpu.make_async_copy(deg, deg_v, loc.at[0])
     get_w = pltpu.make_async_copy(weight, w_v, loc.at[1])
@@ -79,7 +84,7 @@
     get_hw = pltpu.make_async_copy(hub_w, hw_v, loc.at[5])
     for copy in (get_w, get_deg, get_own, get_list):
         copy.start()
-    pl.semaphore_wait(bar, 15)
+    pl.semaphore_wait(bar, 16)
 
     def send1(n, to):
         return pltpu.make_async_remote_copy(
@@ -89,7 +94,7 @@
             device_id=(blk, to), device_id_type=MESH,
         )
 
-    for step, other in NARROW:
+    for step, other in FAR:
         send1(nar, narrow_peer(step, other)).start()
 
     def send_list(step, other):
@@ -100,15 +105,23 @@
             device_id=(yh * 8 + row_peer(4 - step, other), nar), device_id_type=MESH,
         )
 
+    def list_across(g):
+        return pltpu.make_async_remote_copy(
+            src_ref=lists.at[0, 1], dst_ref=lists_v.at[6 + g],
+            send_sem=sl.at[6 + g], recv_sem=rl.at[6 + g],
+            device_id=(chip[g], nar), device_id_type=MESH,
+        )
+
     for step, other in ROW:
         send_list(step, other).start()
+    for g in (2, 3):
+        list_across(g).start()
     get_t(0).start()
     get_t(1).start()
     get_hw.start()
 
     get_w.wait()
     get_deg.wait()
-    wh, wl = split(w_v[...].T)
     inv = lax.rsqrt(deg_v[pl.ds(pl.multiple_of(nar * 8, 8), 8), :].astype(jnp.float32))
 
     position = lax.broadcasted_iota(jnp.int32, (8, TILE), 0) * TILE + lax.broadcasted_iota(
@@ -125,9 +138,10 @@
         return rows
 
     def fill_par(i, rows):
-        for k in range(SLOTS):
-            s = 128 + k // 4 * 32 + i * 4 + k % 4
-            rows = jnp.where(position == s, key((1 - yh) * 8 + i, k, 2000), rows)
+        for first, wide in LEVELS:
+            for k in range(wide):
+                s = 128 + first * 8 + i * wide + k
+                rows = jnp.where(position == s, key((1 - yh) * 8 + i, first + k, 2000), rows)
         return rows
 
     rows = lax.fori_loop(0, 8, fill_own, jnp.zeros((8, TILE), jnp.int32))
@@ -143,16 +157,22 @@
             carry = link(key(yh * 8 + i, k, 1000), i * 16 + k, carry)
         return carry
 
-    def link_par(i, carry):
-        for k in range(SLOTS):
-            o = (1 - yh) * 8 + lax.rem(i, 2) * 4 + k // 4
-            s = 128 + i * 16 + k
-            carry = link(key(o, i // 2 * 4 + k % 4, 1000), s, carry)
-        return carry
+    def link_par(first, wide):
+        def some(i, carry):
+            for j in range(16 // wide):
+                source = i * (16 // wide) + j
+                for k in range(wide):
+                    r = key((1 - yh) * 8 + source, first + k, 1000)
+                    carry = link(r, 128 + first * 8 + source * wide + k, carry)
+            return carry
+
+        return some
 
     carry = jnp.where(rows >= 2000, 0, rows), position
     carry = lax.fori_loop(0, 8, link_own, carry)
-    before, last = lax.fori_loop(0, 8, link_par, carry)
+    for first, wide in LEVELS:
+        carry = lax.fori_loop(0, wide // 2, link_par(first, wide), carry)
+    before, last = carry
     order_v[:8] = before
     order_v[8:] = last
     order_to_smem = pltpu.make_async_copy(order_v, order_s, loc.at[15])
@@ -172,34 +192,43 @@
             get_t(part + 2).start()
     order_to_smem.wait()
 
+    def send2(f, n, to):
+        return pltpu.make_async_remote_copy(
+            src_ref=ysend.at[f, to],
+            dst_ref=y4[f].at[pl.ds(pl.multiple_of(n * 8, 8), 8)],
+            send_sem=s2.at[f, to], recv_sem=r2.at[f, n],
+            device_id=(blk, to), device_id_type=MESH,
+        )
+
+    def own2(f):
+        return pltpu.make_async_copy(
+            ysend.at[f, nar], y4[f].at[pl.ds(pl.multiple_of(nar * 8, 8), 8)], loc.at[6 + f]
+        )
+
+    w_rows = w_v[...].T
+    w_parts = []
+    for f in range(F):
+        hi, lo = split(
+            jnp.concatenate([w_rows[n * 32 + f * 8 : n * 32 + f * 8 + 8] for n in range(8)], axis=0)
+        )
+        w_parts.append((jnp.concatenate([hi, lo], axis=0), hi))
+
     get_own.wait()
     for step, other in NARROW:
         n = narrow_peer(step, other)
         send1(n, n).wait_recv()
-
-    for b in range(8):
-        xh, xl = split(xt[:, b * TILE : (b + 1) * TILE])
-        y = nn_dot(wh, xh) + nn_dot(wl, xh) + nn_dot(wh, xl)
-        y = y * inv[b : b + 1, :]
-        for n in range(8):
-            for f in range(F):
-                row = n * 32 + f * 8
-                ysend[f, n, b] = y[row : row + 8, :]
-
-    def send2(f, n, to):
-        return pltpu.make_async_remote_copy(
-            src_ref=ysend.at[f, to],
-            dst_ref=y4[f].at[pl.ds(pl.multiple_of(n * 8, 8), 8)],
-            send_sem=s2.at[f, to], recv_sem=r2.at[f, n],
-            device_id=(blk, to), device_id_type=MESH,
-        )
-
-    def own2(f):
-        return pltpu.make_async_copy(
-            ysend.at[f, nar], y4[f].at[pl.ds(pl.multiple_of(nar * 8, 8), 8)], loc.at[6 + f]
-        )
-
+    halves_x = [split(xt[:, half * 512 : half * 512 + 512]) for half in range(2)]
     for f in range(F):
+        both, hi = w_parts[f]
+        for half, (xh, xl) in enumerate(halves_x):
+            y = nn_dot(both, xh)
+            y = y[:64] + y[64:] + nn_dot(hi, xl)
+            for b in range(4):
+                scale = inv[half * 4 + b : half * 4 + b + 1, :]
+                for n in range(8):
+                    ysend[f, n, half * 4 + b] = (
+                        y[n * 8 : n * 8 + 8, b * TILE : (b + 1) * TILE] * scale
+                    )
         for step, other in NARROW:
             send2(f, nar, narrow_peer(step, other)).start()
         own2(f).start()
@@ -207,6 +236,8 @@
     get_list.wait()
     for step, other in ROW:
         send_list(step, other).wait_recv()
+    for g in (2, 3):
+        list_across(g).wait_recv()
     to_smem = pltpu.make_async_copy(lists_v, lists_s, loc.at[10])
     to_smem.start()
     to_smem.wait()
@@ -234,8 +265,15 @@
     def send_early(f, source, step, other):
         return send_blocks(early_b, got_early, se, re, f, source, step, other)
 
-    def send_late(q, source, step, other):
-        return send_blocks(late_b, got_late, sq, rq, q, source, step, other)
+    def send_late(level, source, step, other):
+        first, wide = LEVELS[level]
+        slot = step * 2 + other
+        pairs = pl.ds(first // 2, wide // 2)
+        return pltpu.make_async_remote_copy(
+            src_ref=late_b.at[pairs, slot], dst_ref=got_late.at[pairs, source],
+            send_sem=sq.at[level, slot], recv_sem=rq.at[level, source],
+            device_id=(yh * 8 + row_peer(step, other), nar), device_id_type=MESH,
+        )
 
     lane = lax.broadcasted_iota(jnp.int32, (8, TILE), 1)
 
@@ -250,6 +288,28 @@
             src_ref=src, dst_ref=hub_in.at[source], send_sem=sh.at[sem],
             recv_sem=rh.at[source],
             device_id=(yh * 8 + row_peer(step, other), nar), device_id_type=MESH,
+        )
+
+    rows_of = (ya, row1, row2, row3)
+
+    def spread(step):
+        return pltpu.make_async_remote_copy(
+            src_ref=ya, dst_ref=rows_of[step], send_sem=sb.at[step], recv_sem=rb.at[step],
+            device_id=(yh * 8 + row_peer(4 - step, 0), nar), device_id_type=MESH,
+        )
+
+    def relay(step):
+        half = pl.ds(0 if step == 1 else 32, 32)
+        return pltpu.make_async_remote_copy(
+            src_ref=rows_of[step].at[half], dst_ref=row2.at[half],
+            send_sem=sb.at[step - 1], recv_sem=rb.at[step - 1],
+            device_id=(yh * 8 + row_peer(4 - step, 0), nar), device_id_type=MESH,
+        )
+
+    def send_first(g):
+        return pltpu.make_async_remote_copy(
+            src_ref=sel_b.at[g], dst_ref=got_first.at[g], send_sem=sf.at[g], recv_sem=rf.at[g],
+            device_id=(chip[g], nar), device_id_type=MESH,
         )
 
     for f in range(F):
@@ -270,34 +330,59 @@
             swap_hub(blk).start()
             for step, other in ROW:
                 send_hub(hub_v, blk, step * 2 + other, step, other).start()
+        if f == 0:
+            for step in (1, 3):
+                spread(step).start()
+            continue
         send_y(f).start()
         for step, other in ROW:
             slot = step * 2 + other
             for k in range(SLOTS):
-                own_b[f, slot, k] = y4[f][column(slot, blk, k)]
-            send_own(f, me, step, other).start()
+                own_b[f - 1, slot, k] = y4[f][column(slot, blk, k)]
+            send_own(f - 1, me, step, other).start()
         for k in range(SLOTS):
-            got_own[f, me, k] = y4[f][column(0, blk, k)]
+            got_own[f - 1, me, k] = y4[f][column(0, blk, k)]
+        if f == 1:
+            for step in (1, 3):
+                spread(step).wait_recv()
+                relay(step).start()
+
+    for step in (1, 3):
+        relay(step).wait_recv()
+    for g, slot in ((2, 8), (3, 9), (1, 1), (0, 0)):
+        for step in range(4):
+            source = yh * 8 + row_peer(step, 0)
+            for k in range(SLOTS):
+                picked = rows_of[step][column(slot, source, k)]
+                if g == 0:
+                    got_first[g, step, k] = picked
+                else:
+                    sel_b[g, step, k] = picked
+        if g > 0:
+            send_first(g).start()
+
+    def first_at(g, i, k):
+        return got_first[g + lax.rem(i % 2 + core, 2), lax.rem(i // 2 - x + 4, 4), k]
 
     def keep_y(b, carry):
         for f in range(F):
             value[b, f] = y4[f][b]
         return carry
 
-    for f in range(2):
-        send_y(f).wait_recv()
-        for step, other in ROW:
-            slot = step * 2 + other
-            for k in range(SLOTS):
-                early_b[f, slot, k] = yp[f][column(slot, partner, k)]
-            send_early(f, me, step, other).start()
-        for k in range(SLOTS):
-            got_early[f, me, k] = yp[f][column(0, partner, k)]
-
     lax.fori_loop(0, BLOCKS, keep_y, 0)
     swap_hub(partner).wait_recv()
     for step, other in ROW:
         send_hub(hub_in.at[partner], partner, 8 + step * 2 + other, step, other).start()
+
+    send_y(1).wait_recv()
+    for step, other in ROW:
+        slot = step * 2 + other
+        for k in range(SLOTS):
+            early_b[0, slot, k] = yp[1][column(slot, partner, k)]
+        send_early(0, me, step, other).start()
+    for k in range(SLOTS):
+        got_early[0, me, k] = yp[1][column(0, partner, k)]
+
 
     def product(xs, t):
         xh, xl = split(xs)
@@ -322,53 +407,55 @@
         for half in range(2):
             products = []
             for k in range(half * 8, half * 8 + 8):
-                xs = jnp.concatenate([got_own[f, i, k] for f in range(F)], axis=0)
+                xs = jnp.concatenate([first_at(0, i, k)] + [got_own[f, i, k] for f in range(F - 1)], axis=0)
                 products.append(product(xs, my_list[0, 2, yh * 8 + i, k]))
             add(products, i * 16 + half * 8)
         return carry
 
-    def par_products(q):
-        def pair(i, carry):
+    def par_products(first, wide):
+        def some(i, carry):
             products = []
-            for j in range(2):
-                for k in range(4):
+            for j in range(8 // wide):
+                source = i * (8 // wide) + j
+                for k in range(first, first + wide):
                     xs = jnp.concatenate(
-                        [got_early[f, i * 2 + j, q * 4 + k] for f in range(2)]
-                        + [got_late[q, i * 2 + j, f, k] for f in range(2)],
+                        [first_at(2, source, k), got_early[0, source, k]]
+                        + [got_late[k // 2, source, f, k % 2] for f in range(2)],
                         axis=0,
                     )
-                    t = my_list[0, 2, (1 - yh) * 8 + i * 2 + j, q * 4 + k]
-                    products.append(product(xs, t))
-            add(products, 128 + q * 32 + i * 8)
+                    products.append(product(xs, my_list[0, 2, (1 - yh) * 8 + source, k]))
+            add(products, 128 + first * 8 + i * 8)
             return carry
 
-        lax.fori_loop(0, 4, pair, 0)
+        lax.fori_loop(0, wide, some, 0)
 
     for f in range(2, F):
         send_y(f).wait_recv()
 
-    def start_late(q):
+    def start_late(level):
+        first, wide = LEVELS[level]
         for step, other in ROW:
             slot = step * 2 + other
-            for k in range(4):
-                c = column(slot, partner, q * 4 + k)
+            for k in range(first, first + wide):
+                c = column(slot, partner, k)
                 for f in range(2):
-                    late_b[q, slot, f, k] = yp[2 + f][c]
-            send_late(q, me, step, other).start()
-        for k in range(4):
-            c = column(0, partner, q * 4 + k)
+                    late_b[k // 2, slot, f, k % 2] = yp[2 + f][c]
+            send_late(level, me, step, other).start()
+        for k in range(first, first + wide):
+            c = column(0, partner, k)
             for f in range(2):
-                got_late[q, me, f, k] = yp[2 + f][c]
-
-    def late_done(q):
+                got_late[k // 2, me, f, k % 2] = yp[2 + f][c]
+
+    def late_done(level):
         for step, other in ROW:
-            send_late(q, row_peer(step, other), step, other).wait()
-
-    for q in range(4):
-        start_late(q)
-    for f in range(F):
+            send_late(level, row_peer(step, other), step, other).wait()
+
+    for level in range(len(LEVELS)):
+        start_late(level)
+    for f in range(F - 1):
         for step, other in ROW:
             send_own(f, row_peer(step, other), step, other).wait()
+    send_first(1).wait_recv()
     lax.fori_loop(0, 8, own_products, 0)
 
     for step, other in ROW:
@@ -398,7 +485,8 @@
     lax.fori_loop(0, 16, hub_sum, 0)
 
     for f in range(F):
-        send_y(f).wait_send()
+        if f > 0:
+            send_y(f).wait_send()
         for step, other in NARROW:
             n = narrow_peer(step, other)
             send2(f, n, n).wait_send()
@@ -407,16 +495,24 @@
         send1(n, n).wait_send()
     for step, other in ROW:
         send_list(step, other).wait_send()
+    for g in (2, 3):
+        list_across(g).wait_send()
     swap_hub(partner).wait_send()
     for step, other in ROW:
         send_hub(hub_v, blk, step * 2 + other, step, other).wait_send()
         send_hub(hub_v, blk, 8 + step * 2 + other, step, other).wait_send()
-    for f in range(2):
-        for step, other in ROW:
-            send_early(f, row_peer(step, other), step, other).wait()
-    for q in range(4):
-        late_done(q)
-        par_products(q)
+    for step, other in ROW:
+        send_early(0, row_peer(step, other), step, other).wait()
+    for step in (1, 3):
+        spread(step).wait_send()
+        relay(step).wait_send()
+    for g in (1, 2, 3):
+        send_first(g).wait_send()
+    for g in (2, 3):
+        send_first(g).wait_recv()
+    for level in range(len(LEVELS)):
+        late_done(level)
+        par_products(*LEVELS[level])
 
     sub = lax.broadcasted_iota(jnp.int32, (8, TILE), 0)
     biases = []
@@ -439,7 +535,15 @@
                 )
         return carry
 
-    lax.fori_loop(0, 8, finish, 0)
+    def put(i):
+        here = pl.ds(i * 2048, 2048)
+        return pltpu.make_async_copy(out.at[:, here], out_hbm.at[:, here], loc.at[i])
+
+    for i in range(4):
+        lax.fori_loop(i * 2, i * 2 + 2, finish, 0)
+        put(i).start()
+    for i in range(4):
+        put(i).wait()
 
 
 def exchange(feat, deg, weight, lists, counts, hubs, bias, tiles, hub_w):
@@ -453,19 +557,22 @@
         exchange_kernel,
         out_shape=jax.ShapeDtypeStruct((32, BLOCKS * TILE), f32),
         in_specs=[hbm, hbm, hbm, hbm, smem, smem, smem, smem, hbm, hbm],
-        out_specs=pl.BlockSpec(memory_space=vmem),
+        out_specs=hbm,
         scratch_shapes=[
             vmem((256, 1024), f32),
             vmem((F, 8, 8, *tile), f32),
-            *[vmem((BLOCKS, *tile), f32)] * 8,
-            vmem((F, 8, SLOTS, *tile), f32),
-            vmem((2, 8, SLOTS, *tile), f32),
-            vmem((4, 8, 2, 4, *tile), f32),
-            vmem((F, 8, SLOTS, *tile), f32),
-            vmem((2, 8, SLOTS, *tile), f32),
-            vmem((4, 8, 2, 4, *tile), f32),
-            vmem((8, 16, SLOTS), jnp.int32),
-            pltpu.SMEM((8, 16, SLOTS), jnp.int32),
+            *[vmem((BLOCKS, *tile), f32)] * 7,
+            vmem((F - 1, 8, SLOTS, *tile), f32),
+            vmem((1, 8, SLOTS, *tile), f32),
+            vmem((8, 8, 2, 2, *tile), f32),
+            *[vmem((BLOCKS, *tile), f32)] * 3,
+            vmem((4, 4, SLOTS, *tile), f32),
+            vmem((4, 4, SLOTS, *tile), f32),
+            vmem((F - 1, 8, SLOTS, *tile), f32),
+            vmem((1, 8, SLOTS, *tile), f32),
+            vmem((8, 8, 2, 2, *tile), f32),
+            vmem((10, 16, SLOTS), jnp.int32),
+            pltpu.SMEM((10, 16, SLOTS), jnp.int32),
             vmem(tile, f32),
             vmem((16, *tile), f32),
             vmem((BLOCKS, TILE), jnp.int32),
@@ -477,14 +584,17 @@
             pltpu.SMEM((16, TILE), jnp.int32),
             vmem((BLOCKS + TV, F, *tile), f32),
             vmem((BLOCKS, F, *tile), f32),
+            vmem((32, BLOCKS * TILE), f32),
             dma((8,)), dma((8,)),
             dma((F, 8)), dma((F, 8)),
             dma((F,)), dma((F,)),
-            dma((8,)), dma((8,)),
+            dma((10,)), dma((10,)),
             dma((17,)), dma((16,)),
-            dma((F, 8)), dma((F, 8)),
-            dma((2, 8)), dma((2, 8)),
-            dma((4, 8)), dma((4, 8)),
+            dma((F - 1, 8)), dma((F - 1, 8)),
+            dma((1, 8)), dma((1, 8)),
+            dma((len(LEVELS), 8)), dma((len(LEVELS), 8)),
+            dma((4,)), dma((4,)),
+            dma((4,)), dma((4,)),
             dma((16,)),
         ],
         compiler_params=pltpu.CompilerParams(

time: 83 us -> 81.7 us (0.984)
  Pallas kernels: 80.5 us -> 79.2 us
    pallas_call x1, Pallas kernels: 80.5 us -> 79.2 us  [exchange(): pl.pallas_call(exchange_kernel, out_shape=jax.ShapeDtypeStruct((32, BLOCK...]
where the time goes in v5:
time: 81.7 us; the launch traced here: 81.5 us
  Pallas kernels  79.2 us (97%)
  local copies, waits for them, and re-layouts  2.26 us (3%)
    pallas_call x1, Pallas kernels, exchange(): pl.pallas_call(exchange_kernel, out_shape=jax.ShapeDtypeStruct((32, BLOCK...  79.2 us
    unnamed x1, local copies, waits for them, and re-layouts  2.26 us

profile of v5, /device:TPU:1, one launch (start us, length us, event | category | flops | bytes accessed | tf_op | source)
XLA Modules:
  0.0 81.5 jit_solution(11108744298450189754)
XLA Ops:
  0.0 79.2 %shard_map.91 = f32[32,8192]{1,0:T(8,128)} custom-call(f32[32,8192]{1,0:T(8,128)} %feat.1, s32[64,128]{1,0:T(8,128)} %bitcast.4, f32[256,256]{1,0:T(8,128)} %weight.1, s32[1,3,16,16]{3,2,1,0:T(8,128)} %bitcast.2, s32[1,3,16,16]{3,2,1,0:T(8,128)} %bitcast.3, s32[1,16]{1,0:T(1,128)} %counts.1, s32[1,8]{1,0:T(1,128)} %hubs.1, f32[256]{0:T(256)} %bias.1, ...), custom_call_target="tpu_custom_call" | custom-call | tf_op jit(solution)/shard_map/pallas_call | solution.py:556
  79.3 2.3 %copy.11 = f32[32,8192]{1,0:T(8,128)} copy(f32[32,8192]{1,0:T(8,128)} %shard_map.91) | data formatting | bytes 2097152

commit v6 on v5

--- a/solution.py
+++ b/solution.py
@@ -555,7 +555,7 @@
     tile = (8, TILE)
     return pl.pallas_call(
         exchange_kernel,
-        out_shape=jax.ShapeDtypeStruct((32, BLOCKS * TILE), f32),
+        out_shape=pltpu.VMEM((32, BLOCKS * TILE), f32),
         in_specs=[hbm, hbm, hbm, hbm, smem, smem, smem, smem, hbm, hbm],
         out_specs=hbm,
         scratch_shapes=[

time: 81.7 us -> 79.7 us (0.976)
  local copies, waits for them, and re-layouts: 2.26 us -> 0.97 us
    unnamed x1, local copies, waits for them, and re-layouts: 2.26 us -> 0.97 us
where the time goes in v6:
time: 79.7 us; the launch traced here: 79.5 us
  Pallas kernels  78.6 us (99%)
  local copies, waits for them, and re-layouts  0.97 us (1%)
    pallas_call x1, Pallas kernels, exchange(): pl.pallas_call(exchange_kernel, out_shape=pltpu.VMEM((32, BLOCKS * TILE),...  78.6 us

profile of v6, /device:TPU:1, one launch (start us, length us, event | category | flops | bytes accessed | tf_op | source)
XLA Modules:
  0.0 79.5 jit_solution(15877990172812916072)
XLA Ops:
  0.0 78.6 %shard_map.91 = f32[32,8192]{1,0:T(8,128)S(1)} custom-call(f32[32,8192]{1,0:T(8,128)} %feat.1, s32[64,128]{1,0:T(8,128)} %bitcast.4, f32[256,256]{1,0:T(8,128)} %weight.1, s32[1,3,16,16]{3,2,1,0:T(8,128)} %bitcast.2, s32[1,3,16,16]{3,2,1,0:T(8,128)} %bitcast.3, s32[1,16]{1,0:T(1,128)} %counts.1, s32[1,8]{1,0:T(1,128)} %hubs.1, f32[256]{0:T(256)} %bias.1, ...), custom_call_target="tpu_custom_call" | custom-call | tf_op jit(solution)/shard_map/pallas_call | solution.py:556
  78.6 1.0 %copy.11 = f32[32,8192]{1,0:T(8,128)} copy(f32[32,8192]{1,0:T(8,128)S(1)} %shard_map.91) | data formatting | bytes 2097152

commit v7 on v6

--- a/solution.py
+++ b/solution.py
@@ -14,7 +14,7 @@
 TV = 256
 LEVELS = ((0, 4), (4, 4), (8, 4), (12, 2), (14, 2))
 MESH = pl.DeviceIdType.MESH
-ROW = ((2, 0), (2, 1), (1, 0), (3, 0), (1, 1), (3, 1), (0, 1))
+ROW = ((1, 0), (3, 0), (1, 1), (3, 1), (2, 0), (2, 1), (0, 1))
 FAR = ((2, 1), (1, 1), (3, 1), (0, 1), (2, 0), (1, 0), (3, 0))
 NARROW = ((1, 0), (3, 0), (0, 1), (2, 0), (1, 1), (3, 1), (2, 1))
 
@@ -35,11 +35,11 @@
 
 def exchange_kernel(
     feat, deg, weight, lists, my_list, counts, hubs, bias, tiles, hub_w,
-    out_hbm,
+    out,
     xt, ysend, ya, yb, yc, yd, pb, pc, pd, own_b, early_b, late_b,
     row1, row2, row3, sel_b, got_first,
     got_own, got_early, got_late, lists_v, lists_s, hub_v, hub_in, deg_v, w_v, raw_t, t_v, hw_v,
-    order_v, order_s, value, hub_sums, out,
+    order_v, order_s, value, hub_sums,
     s1, r1, s2, r2, sy, ry, sl, rl, sh, rh, so, ro, se, re, sq, rq, sb, rb, sf, rf, loc,
 ):
     y4, yp = (ya, yb, yc, yd), (None, pb, pc, pd)
@@ -535,15 +535,7 @@
                 )
         return carry
 
-    def put(i):
-        here = pl.ds(i * 2048, 2048)
-        return pltpu.make_async_copy(out.at[:, here], out_hbm.at[:, here], loc.at[i])
-
-    for i in range(4):
-        lax.fori_loop(i * 2, i * 2 + 2, finish, 0)
-        put(i).start()
-    for i in range(4):
-        put(i).wait()
+    lax.fori_loop(0, 8, finish, 0)
 
 
 def exchange(feat, deg, weight, lists, counts, hubs, bias, tiles, hub_w):
@@ -557,7 +549,7 @@
         exchange_kernel,
         out_shape=pltpu.VMEM((32, BLOCKS * TILE), f32),
         in_specs=[hbm, hbm, hbm, hbm, smem, smem, smem, smem, hbm, hbm],
-        out_specs=hbm,
+        out_specs=pl.BlockSpec(memory_space=vmem),
         scratch_shapes=[
             vmem((256, 1024), f32),
             vmem((F, 8, 8, *tile), f32),
@@ -584,7 +576,6 @@
             pltpu.SMEM((16, TILE), jnp.int32),
             vmem((BLOCKS + TV, F, *tile), f32),
             vmem((BLOCKS, F, *tile), f32),
-            vmem((32, BLOCKS * TILE), f32),
             dma((8,)), dma((8,)),
             dma((F, 8)), dma((F, 8)),
             dma((F,)), dma((F,)),

time: 79.7 us -> 78.3 us (0.982)
  Pallas kernels: 78.6 us -> 77.2 us
    pallas_call x1, Pallas kernels: 78.6 us -> 77.2 us  [exchange(): pl.pallas_call(exchange_kernel, out_shape=pltpu.VMEM((32, BLOCKS * TILE),...]
where the time goes in v7:
time: 78.3 us; the launch traced here: 78.1 us
  Pallas kernels  77.2 us (99%)
  local copies, waits for them, and re-layouts  0.97 us (1%)
    pallas_call x1, Pallas kernels, exchange(): pl.pallas_call(exchange_kernel, out_shape=pltpu.VMEM((32, BLOCKS * TILE),...  77.2 us

profile of v7, /device:TPU:1, one launch (start us, length us, event | category | flops | bytes accessed | tf_op | source)
XLA Modules:
  0.0 78.1 jit_solution(3023635457981765138)
XLA Ops:
  0.0 77.2 %shard_map.91 = f32[32,8192]{1,0:T(8,128)S(1)} custom-call(f32[32,8192]{1,0:T(8,128)} %feat.1, s32[64,128]{1,0:T(8,128)} %bitcast.4, f32[256,256]{1,0:T(8,128)} %weight.1, s32[1,3,16,16]{3,2,1,0:T(8,128)} %bitcast.2, s32[1,3,16,16]{3,2,1,0:T(8,128)} %bitcast.3, s32[1,16]{1,0:T(1,128)} %counts.1, s32[1,8]{1,0:T(1,128)} %hubs.1, f32[256]{0:T(256)} %bias.1, ...), custom_call_target="tpu_custom_call" | custom-call | tf_op jit(solution)/shard_map/pallas_call | solution.py:548
  77.2 1.0 %copy.11 = f32[32,8192]{1,0:T(8,128)} copy(f32[32,8192]{1,0:T(8,128)S(1)} %shard_map.91) | data formatting | bytes 2097152
